TPU v7x, 32 devices: a whole 2x2x4 slice. The times are simulated.
32 devices in a mesh: dp: 4 (over z), ctx: 2 (over x), tensor: 4 (over y, core).
Axes of the slice: x: 2, y: 2, z: 4, core: 2. Of those that a mesh axis runs over, the one named last changes fastest.
Arguments:
- inputs: bfloat16 [8, 1024, 768], P('dp', 'ctx'), may hold values from -6 to 6
- lengths: int32 [8], P('dp'), may hold values from 256 to 1024, as said below
- expert_ids: int32 [8, 1024], P('dp', 'ctx'), may hold values from 0 to 3, as said below
- slot_rows: int32 [8, 2, 4, 256], P('dp', 'ctx'), may hold values from 0 to 512, as said below
- attn_gain: bfloat16 [768], P(('dp', 'ctx')), may hold values from 0.5 to 1.5
- qkv_weight: bfloat16 [3, 768, 768], P(None, ('dp', 'ctx'), 'tensor'), may hold values from -0.21875 to 0.21875
- out_weight: bfloat16 [768, 768], P('tensor', ('dp', 'ctx')), may hold values from -1.75 to 1.75
- position_bias: float32 [32, 12], P(None, 'tensor'), may hold values from -3 to 3
- ffn_gain: bfloat16 [768], P(('dp', 'ctx')), may hold values from 0.5 to 1.5
- router_weight: bfloat16 [768, 4], P(('dp', 'ctx')), may hold values from -0.125 to 0.125
- up_weight: bfloat16 [4, 768, 3072], P(None, ('dp', 'ctx'), 'tensor'), may hold values from -0.21875 to 0.21875
- down_weight: bfloat16 [4, 3072, 768], P(None, 'tensor', ('dp', 'ctx')), may hold values from -0.875 to 0.875
- cotangent: bfloat16 [8, 1024, 768], P('dp', 'ctx'), may hold values from -6 to 6
Outputs:
- outputs: bfloat16 [8, 1024, 768], P('dp', 'ctx')
- input_grad: bfloat16 [8, 1024, 768], P('dp', 'ctx')
- attn_gain_grad: float32 [768], P(('dp', 'ctx'))
- qkv_grad: float32 [3, 768, 768], P(None, ('dp', 'ctx'), 'tensor')
- out_proj_grad: float32 [768, 768], P('tensor', ('dp', 'ctx'))
- bias_table_grad: float32 [32, 12], P(None, 'tensor')
- ffn_gain_grad: float32 [768], P(('dp', 'ctx'))
- router_grad: float32 [768, 4], P(('dp', 'ctx'))
- up_grad: float32 [4, 768, 3072], P(None, ('dp', 'ctx'), 'tensor')
- down_grad: float32 [4, 3072, 768], P(None, 'tensor', ('dp', 'ctx'))
Inputs may be any that keep to these rules, and one draw needn't show every extreme that they name: `lengths`: in each group of 2 sequences that one index of dp holds, one has length 1024; some sequence has length 256. `expert_ids`: position t's expert is the expert in whose slots of t's segment it stands in slot_rows. `slot_rows`: entries are positions within the segment; 512 marks an empty slot. Every position of a segment stands in exactly one slot, and in every segment one expert fills all 256 of its slots.
All inputs are finite; a program needn't handle non-finite values.
Results may differ from a plain program's by a relative error of at most 0.025.
Values may be sent and summed in bfloat16 or wider, within the bound.
A program may use at most 384 MiB of HBM per device.

v0:
```python
import jax
import jax.numpy as jnp
import numpy as np
from jax import lax
from jax.sharding import PartitionSpec as P

BUCKETS = 32


bucket_edges = np.ceil(16.0 * 8.0 ** (np.arange(1, 16) / 16.0)).astype(np.int32)


def bucket_of(distance):
    clipped = jnp.maximum(distance, 0)
    edge_values = jnp.asarray(bucket_edges, dtype=jnp.int32)
    beyond = jnp.sum((clipped[..., None] >= edge_values).astype(jnp.int32), axis=-1)
    return jnp.where(clipped < 16, clipped, jnp.minimum(16 + beyond, 31))


def rms_norm(values, gain_vector):
    return (
        values * lax.rsqrt(jnp.mean(values * values, axis=-1, keepdims=True) + 1e-06) * gain_vector
    )


def toeplitz(diagonal, query_count, key_count):
    head_count = diagonal.shape[0]
    padded = jnp.pad(diagonal, ((0, 0), (0, 1)))
    row_width = query_count + key_count
    repeated = jnp.broadcast_to(padded[:, None, :], (head_count, query_count, row_width)).reshape(
        head_count, query_count * row_width
    )
    repeated = jnp.pad(repeated, ((0, 0), (0, query_count))).reshape(
        head_count, query_count, row_width + 1
    )[:, :, :key_count]
    return repeated[:, :, ::-1]


def diagonal_sums(gradient):
    head_count, query_count, key_count = gradient.shape
    offset_count = query_count + key_count - 1
    flipped = jnp.pad(gradient[:, :, ::-1], ((0, 0), (0, 0), (0, query_count)))
    skewed = flipped.reshape(head_count, query_count * (offset_count + 1))[
        :, : query_count * offset_count
    ]
    return jnp.sum(skewed.reshape(head_count, query_count, offset_count), axis=1)


def bucket_table(query_first, query_count, key_count):
    offsets = (
        query_first - (key_count - 1) + jnp.arange(query_count + key_count - 1, dtype=jnp.int32)
    )
    return (bucket_of(offsets)[:, None] == jnp.arange(BUCKETS, dtype=jnp.int32)[None, :]).astype(
        jnp.float32
    )


def body(
    inputs,
    lengths,
    expert_ids,
    slot_rows,
    attn_gain,
    qkv_weight,
    out_weight,
    position_bias,
    ffn_gain,
    router_weight,
    up_weight,
    down_weight,
    cotangent,
):
    highest = lax.Precision.HIGHEST
    micro_count, seg_rows, model_width = inputs.shape
    local_heads = position_bias.shape[1]
    head_size = qkv_weight.shape[2] // local_heads
    expert_count = up_weight.shape[0]
    query_first = lax.axis_index("ctx") * seg_rows
    query_pos = query_first + jnp.arange(seg_rows, dtype=jnp.int32)

    def pair_scores(query_heads, query_start, key_heads, length):
        query_count = query_heads.shape[0]
        key_count = key_heads.shape[0]
        scores = (
            jnp.einsum("qhd,khd->hqk", query_heads, key_heads, preferred_element_type=jnp.float32)
            * 0.125
        )
        diagonal = jnp.einsum(
            "rb,bh->hr",
            bucket_table(query_start, query_count, key_count),
            position_bias,
            precision=highest,
        )
        scores = scores + toeplitz(diagonal, query_count, key_count)
        query_place = query_start + jnp.arange(query_count, dtype=jnp.int32)
        key_place = jnp.arange(key_count, dtype=jnp.int32)
        allowed = (key_place[None, :] <= query_place[:, None]) & (key_place[None, :] < length)
        return (scores, allowed)

    def scores_for(query_heads, key_block, length):
        key_count = key_block.shape[0]
        key_heads = key_block.reshape(key_count, local_heads, head_size)
        scores, allowed = pair_scores(query_heads, query_first, key_heads, length)
        return (scores, allowed, key_heads)

    results = []
    input_parts = []
    grad_sums = None
    bias_total = jnp.zeros((local_heads, BUCKETS), jnp.float32)
    for micro_step in range(micro_count):
        forward_gain_one = lax.all_gather(attn_gain, ("dp", "ctx"), axis=0, tiled=True)
        forward_qkv_full = lax.all_gather(qkv_weight, ("dp", "ctx"), axis=1, tiled=True)
        forward_out_full = lax.all_gather(out_weight, ("dp", "ctx"), axis=1, tiled=True)
        forward_gain_two = lax.all_gather(ffn_gain, ("dp", "ctx"), axis=0, tiled=True)
        forward_router_full = lax.all_gather(router_weight, ("dp", "ctx"), axis=0, tiled=True)
        forward_up_full = lax.all_gather(up_weight, ("dp", "ctx"), axis=1, tiled=True)
        forward_down_full = lax.all_gather(down_weight, ("dp", "ctx"), axis=2, tiled=True)
        forward_tokens = inputs[micro_step].astype(jnp.float32)
        forward_length = lengths[micro_step]
        forward_normed = rms_norm(forward_tokens, forward_gain_one.astype(jnp.float32)).astype(
            jnp.bfloat16
        )
        forward_projected = jnp.einsum(
            "td,cde->cte", forward_normed, forward_qkv_full, preferred_element_type=jnp.float32
        ).astype(jnp.bfloat16)
        forward_query_heads = forward_projected[0].reshape(seg_rows, local_heads, head_size)
        row_top = jnp.full((local_heads, seg_rows), -1e30, jnp.float32)
        attend_scores, attend_allowed, attend_key_heads = scores_for(
            forward_query_heads,
            lax.all_gather(forward_projected[1], "ctx", axis=0, tiled=True),
            forward_length,
        )
        value_heads = lax.all_gather(forward_projected[2], "ctx", axis=0, tiled=True).reshape(
            attend_key_heads.shape
        )
        attend_scores = jnp.where(attend_allowed[None], attend_scores, -1e30)
        new_top = jnp.maximum(row_top, jnp.max(attend_scores, axis=-1))
        weights_exp = jnp.where(
            attend_allowed[None], jnp.exp(attend_scores - new_top[:, :, None]), 0.0
        )
        row_total = jnp.sum(weights_exp, axis=-1)
        summed = jnp.einsum(
            "hqk,khd->hqd",
            weights_exp.astype(jnp.bfloat16),
            value_heads,
            preferred_element_type=jnp.float32,
        )
        row_top, row_total, summed = (new_top, row_total, summed)
        forward_attended = summed / row_total[:, :, None]
        forward_log_total = row_top + jnp.log(row_total)
        forward_attended_low = (
            jnp.transpose(forward_attended, (1, 0, 2)).reshape(seg_rows, -1).astype(jnp.bfloat16)
        )
        branch = lax.psum(
            jnp.dot(
                forward_attended_low, forward_out_full, preferred_element_type=jnp.float32
            ).astype(jnp.bfloat16),
            "tensor",
        ).astype(jnp.float32)
        forward_hidden = forward_tokens + branch
        forward_normed_two = rms_norm(forward_hidden, forward_gain_two.astype(jnp.float32)).astype(
            jnp.bfloat16
        )
        logits = jnp.dot(
            forward_normed_two, forward_router_full, preferred_element_type=jnp.float32
        )
        forward_router_probs = jax.nn.softmax(logits, axis=-1)
        forward_chosen = (
            expert_ids[micro_step][:, None] == jnp.arange(expert_count, dtype=jnp.int32)[None, :]
        ).astype(jnp.float32)
        forward_gate_value = jnp.sum(forward_router_probs * forward_chosen, axis=-1)
        forward_slot_table = slot_rows[micro_step, 0]
        padded = jnp.concatenate(
            [forward_normed_two, jnp.zeros((1, model_width), jnp.bfloat16)], axis=0
        )
        forward_picked = padded[forward_slot_table]
        forward_raised = jnp.einsum(
            "ekd,edf->ekf", forward_picked, forward_up_full, preferred_element_type=jnp.float32
        )
        forward_activated = jax.nn.gelu(forward_raised).astype(jnp.bfloat16)
        lowered = jnp.einsum(
            "ekf,efd->ekd", forward_activated, forward_down_full, preferred_element_type=jnp.float32
        )
        spread = (
            jnp.zeros((seg_rows + 1, model_width), jnp.float32)
            .at[forward_slot_table.reshape(-1)]
            .add(lowered.reshape(-1, model_width))[:seg_rows]
        )
        forward_expert_sum = lax.psum(spread.astype(jnp.bfloat16), "tensor").astype(jnp.float32)
        forward_live_rows = (query_pos < forward_length).astype(jnp.float32)[:, None]
        result = (
            forward_live_rows * (forward_hidden + forward_gate_value[:, None] * forward_expert_sum)
        ).astype(jnp.bfloat16)
        forward_kept_state = (
            forward_tokens,
            forward_length,
            forward_normed,
            forward_projected,
            forward_attended,
            forward_log_total,
            forward_attended_low,
            forward_hidden,
            forward_normed_two,
            forward_router_probs,
            forward_chosen,
            forward_gate_value,
            forward_slot_table,
            forward_picked,
            forward_raised,
            forward_activated,
            forward_expert_sum,
            forward_live_rows,
        )
        result, kept_state = (result, forward_kept_state)
        gain_one = lax.all_gather(attn_gain, ("dp", "ctx"), axis=0, tiled=True)
        qkv_full = lax.all_gather(qkv_weight, ("dp", "ctx"), axis=1, tiled=True)
        out_full = lax.all_gather(out_weight, ("dp", "ctx"), axis=1, tiled=True)
        gain_two = lax.all_gather(ffn_gain, ("dp", "ctx"), axis=0, tiled=True)
        router_full = lax.all_gather(router_weight, ("dp", "ctx"), axis=0, tiled=True)
        up_full = lax.all_gather(up_weight, ("dp", "ctx"), axis=1, tiled=True)
        down_full = lax.all_gather(down_weight, ("dp", "ctx"), axis=2, tiled=True)
        (
            tokens,
            backward_length,
            normed,
            projected,
            attended,
            log_total,
            attended_low,
            hidden,
            normed_two,
            router_probs,
            chosen,
            gate_value,
            slot_table,
            picked,
            raised,
            activated,
            expert_sum,
            live_rows,
        ) = kept_state
        upstream = live_rows * cotangent[micro_step].astype(jnp.float32)
        sum_grad = (gate_value[:, None] * upstream).astype(jnp.bfloat16)
        gate_grad = jnp.sum(expert_sum * upstream, axis=-1)
        logit_grad = (router_probs * gate_grad[:, None] * (chosen - gate_value[:, None])).astype(
            jnp.bfloat16
        )
        router_part = jnp.einsum(
            "td,te->de", normed_two, logit_grad, preferred_element_type=jnp.float32
        )
        padded_grad = jnp.concatenate([sum_grad, jnp.zeros((1, model_width), jnp.bfloat16)], axis=0)
        slot_grad = padded_grad[slot_table]
        down_part = jnp.einsum(
            "ekf,ekd->efd", activated, slot_grad, preferred_element_type=jnp.float32
        )
        act_grad = jnp.einsum(
            "ekd,efd->ekf", slot_grad, down_full, preferred_element_type=jnp.float32
        )
        unused_value, gelu_back = jax.vjp(jax.nn.gelu, raised)
        raised_grad = gelu_back(act_grad)[0].astype(jnp.bfloat16)
        up_part = jnp.einsum(
            "ekd,ekf->edf", picked, raised_grad, preferred_element_type=jnp.float32
        )
        picked_grad = jnp.einsum(
            "ekf,edf->ekd", raised_grad, up_full, preferred_element_type=jnp.float32
        )
        spread_grad = (
            jnp.zeros((seg_rows + 1, model_width), jnp.float32)
            .at[slot_table.reshape(-1)]
            .add(picked_grad.reshape(-1, model_width))[:seg_rows]
        )
        normed_two_grad = lax.psum(spread_grad.astype(jnp.bfloat16), "tensor").astype(
            jnp.float32
        ) + jnp.einsum("te,de->td", logit_grad, router_full, preferred_element_type=jnp.float32)
        unused_norm, second_back = jax.vjp(rms_norm, hidden, gain_two.astype(jnp.float32))
        hidden_grad, gain_two_part = second_back(normed_two_grad)
        hidden_grad = hidden_grad + upstream
        branch_grad = hidden_grad.astype(jnp.bfloat16)
        out_part = jnp.einsum(
            "te,td->ed", attended_low, branch_grad, preferred_element_type=jnp.float32
        )
        attended_grad = jnp.einsum(
            "td,ed->te", branch_grad, out_full, preferred_element_type=jnp.float32
        ).astype(jnp.bfloat16)
        grad_heads = attended_grad.reshape(seg_rows, local_heads, head_size)
        row_delta = jnp.sum(
            jnp.transpose(grad_heads.astype(jnp.float32), (1, 0, 2)) * attended, axis=-1
        )
        backward_query_heads = projected[0].reshape(seg_rows, local_heads, head_size)
        bias_zero = jnp.zeros((local_heads, BUCKETS), jnp.float32)
        attend_bias_acc = bias_zero
        bias_acc = attend_bias_acc
        score_scores, score_allowed, score_key_heads = scores_for(
            backward_query_heads,
            lax.all_gather(projected[1], "ctx", axis=0, tiled=True),
            backward_length,
        )
        score_value_heads = lax.all_gather(projected[2], "ctx", axis=0, tiled=True).reshape(
            score_key_heads.shape
        )
        score_key_count = score_key_heads.shape[0]
        soft_weights = jnp.where(
            score_allowed[None], jnp.exp(score_scores - log_total[:, :, None]), 0.0
        )
        weight_grad = jnp.einsum(
            "qhd,khd->hqk", grad_heads, score_value_heads, preferred_element_type=jnp.float32
        )
        score_grad = (soft_weights * (weight_grad - row_delta[:, :, None])).astype(jnp.bfloat16)
        query_acc = jnp.einsum(
            "hqk,khd->qhd", score_grad, score_key_heads, preferred_element_type=jnp.float32
        )
        bias_acc = bias_acc + jnp.dot(
            diagonal_sums(score_grad.astype(jnp.float32)),
            bucket_table(query_first, seg_rows, score_key_count),
            precision=highest,
        )
        (
            (attend_query_acc, attend_bias_acc),
            attend_soft_weights,
            attend_score_grad,
            attend_key_count,
        ) = ((query_acc, bias_acc), soft_weights, score_grad, score_key_count)
        key_term = (
            jnp.einsum(
                "hqk,qhd->khd",
                attend_score_grad,
                backward_query_heads,
                preferred_element_type=jnp.float32,
            )
            * 0.125
        )
        value_term = jnp.einsum(
            "hqk,qhd->khd",
            attend_soft_weights.astype(jnp.bfloat16),
            grad_heads,
            preferred_element_type=jnp.float32,
        )
        grad_term = jnp.stack(
            [key_term.reshape(attend_key_count, -1), value_term.reshape(attend_key_count, -1)],
            axis=1,
        )
        key_value_acc = grad_term
        query_acc, key_value_acc, bias_part = (attend_query_acc, key_value_acc, attend_bias_acc)
        own_grads = lax.psum_scatter(
            key_value_acc.astype(jnp.bfloat16), "ctx", scatter_dimension=0, tiled=True
        ).astype(jnp.float32)
        query_grad = (query_acc * 0.125).reshape(seg_rows, -1).astype(jnp.bfloat16)
        qkv_grad = jnp.stack(
            [
                query_grad,
                own_grads[:, 0].astype(jnp.bfloat16),
                own_grads[:, 1].astype(jnp.bfloat16),
            ],
            axis=0,
        )
        qkv_part = jnp.einsum("td,cte->cde", normed, qkv_grad, preferred_element_type=jnp.float32)
        normed_grad = lax.psum(
            jnp.einsum(
                "cte,cde->td", qkv_grad, qkv_full, preferred_element_type=jnp.float32
            ).astype(jnp.bfloat16),
            "tensor",
        ).astype(jnp.float32)
        unused_first, first_back = jax.vjp(rms_norm, tokens, gain_one.astype(jnp.float32))
        token_grad, gain_one_part = first_back(normed_grad)
        input_part = (token_grad + hidden_grad).astype(jnp.bfloat16)
        weight_parts = (
            gain_one_part,
            qkv_part,
            out_part,
            gain_two_part,
            router_part,
            up_part,
            down_part,
        )
        input_part, weight_parts, bias_part = (input_part, weight_parts, bias_part)
        results.append(result)
        input_parts.append(input_part)
        grad_sums = (
            weight_parts
            if grad_sums is None
            else tuple((old_sum + new_part for old_sum, new_part in zip(grad_sums, weight_parts)))
        )
        bias_total = bias_total + bias_part
    reduced = (
        lax.psum_scatter(grad_sums[0], ("dp", "ctx"), scatter_dimension=0, tiled=True),
        lax.psum_scatter(grad_sums[1], ("dp", "ctx"), scatter_dimension=1, tiled=True),
        lax.psum_scatter(grad_sums[2], ("dp", "ctx"), scatter_dimension=1, tiled=True),
        lax.psum_scatter(grad_sums[3], ("dp", "ctx"), scatter_dimension=0, tiled=True),
        lax.psum_scatter(grad_sums[4], ("dp", "ctx"), scatter_dimension=0, tiled=True),
        lax.psum_scatter(grad_sums[5], ("dp", "ctx"), scatter_dimension=1, tiled=True),
        lax.psum_scatter(grad_sums[6], ("dp", "ctx"), scatter_dimension=2, tiled=True),
    )
    bias_grad_total = lax.psum(bias_total, ("dp", "ctx"))
    return (
        jnp.stack(results, axis=0),
        jnp.stack(input_parts, axis=0),
        reduced[0],
        reduced[1],
        reduced[2],
        jnp.transpose(bias_grad_total),
        reduced[3],
        reduced[4],
        reduced[5],
        reduced[6],
    )


def solution(mesh):
    return jax.shard_map(
        body,
        mesh=mesh,
        in_specs=(
            P("dp", "ctx", None),
            P("dp"),
            P("dp", "ctx"),
            P("dp", "ctx", None, None),
            P(("dp", "ctx")),
            P(None, ("dp", "ctx"), "tensor"),
            P("tensor", ("dp", "ctx")),
            P(None, "tensor"),
            P(("dp", "ctx")),
            P(("dp", "ctx"), None),
            P(None, ("dp", "ctx"), "tensor"),
            P(None, "tensor", ("dp", "ctx")),
            P("dp", "ctx", None),
        ),
        out_specs=(
            P("dp", "ctx", None),
            P("dp", "ctx", None),
            P(("dp", "ctx")),
            P(None, ("dp", "ctx"), "tensor"),
            P("tensor", ("dp", "ctx")),
            P(None, "tensor"),
            P(("dp", "ctx")),
            P(("dp", "ctx"), None),
            P(None, ("dp", "ctx"), "tensor"),
            P(None, "tensor", ("dp", "ctx")),
        ),
        check_vma=False,
    )
```

profile of v0, /device:TPU:0, one launch (start us, length us, event | category | flops | bytes accessed | tf_op | source)
XLA Modules:
  0.0 1232.2 jit_solution(16362353304003233795)
XLA Ops:
  13.7 23.7 %all-reduce.19 = (bf16[768]{0:T(1024)(128)(2,1)S(1)}, bf16[768]{0:T(1024)(128)(2,1)}) all-reduce(bf16[768]{0:T(1024)(128)(2,1)S(1)} %dynamic-update-slice, bf16[768]{0:T(1024)(128)(2,1)S(1)} %dynamic-update-slice.1), channel_id=1, replica_groups=mesh['dp'=4,'ctx'=2,'tensor'=4] {'dp','ctx'}, use_global_device_ids=true, to_apply=%add.14 | all-reduce | flops 1536 | bytes 6144
  42.2 31.0 %all_gather.26 = bf16[192,768]{0,1:T(8,128)(2,1)S(1)} all-gather(bf16[192,96]{0,1:T(8,128)(2,1)S(1)} %copy.60), channel_id=1, replica_groups=mesh['dp'=4,'ctx'=2,'tensor'=4] {'dp','ctx'}, dimensions={1}, use_global_device_ids=true | all-gather | bytes 331776 | tf_op jit(solution)/shard_map/all_gather | solution.py:113
  73.2 34.0 %all_gather.23 = bf16[3,768,192]{2,0,1:T(4,128)(2,1)S(1)} all-gather(bf16[3,96,192]{2,0,1:T(4,128)(2,1)S(1)} %copy.58), channel_id=1, replica_groups=mesh['dp'=4,'ctx'=2,'tensor'=4] {'dp','ctx'}, dimensions={1}, use_global_device_ids=true | all-gather | bytes 995328 | tf_op jit(solution)/shard_map/all_gather | solution.py:112
  111.3 7.3 all-gather.2
  140.5 19.9 %copy.81 = f32[1,3,512,1536]{3,1,2,0:T(4,128)S(1)} copy(f32[1,3,512,1536]{3,2,1,0:T(8,128)S(1)} %broadcast_bitcast_fusion) | data formatting | bytes 18874368
  165.2 13.2 %reshape.676 = f32[2360832]{0:T(1024)} reshape(f32[3,786944]{1,0:T(4,128)} %pad.38) | data formatting | bytes 18886656
  178.4 16.8 %reshape.540 = f32[3,512,1537]{2,1,0:T(8,128)} reshape(f32[2360832]{0:T(1024)} %reshape.676) | data formatting | bytes 18886656 | tf_op jit(solution)/shard_map/reshape | solution.py:33
  195.2 6.5 slice.144
  201.7 51.0 %rev.18 = f32[3,512,1024]{2,1,0:T(8,128)} reverse(f32[3,512,1024]{2,1,0:T(8,128)} %slice.144), dimensions={2} | reverse | bytes 12582912 | tf_op jit(solution)/shard_map/rev | solution.py:36
  261.7 14.4 %fusion.4 = f32[3,512]{1,0:T(4,128)S(1)} fusion(f32[3,512,1024]{2,1,0:T(8,128)S(1)} %get-tuple-element.122, f32[3,512]{1,0:T(4,128)S(1)} %broadcast_maximum_fusion, pred[512,1024]{1,0:T(8,128)(4,1)S(1)} %get-tuple-element.111), kind=kLoop, calls=%fused_computation.24 | loop fusion | flops 6289920 | bytes 6828032 | tf_op jit(solution)/shard_map/reduce_sum | solution.py:141
  288.1 19.2 %all-gather.4 = bf16[8,96,4]{1,2,0:T(4,128)(2,1)S(1)} all-gather(bf16[1,96,4]{1,2,0:T(4,128)(2,1)S(1)} %bitcast.327), channel_id=1, replica_groups=mesh['dp'=4,'ctx'=2,'tensor'=4] {'dp','ctx'}, dimensions={0}, use_global_device_ids=true | all-gather | bytes 6912 | tf_op jit(solution)/shard_map/all_gather | solution.py:115
  308.8 20.7 %all-reduce.31.cloned.1.call-done = (bf16[512,768]{1,0:T(8,128)(2,1)}, bf16[512,768]{1,0:T(8,128)(2,1)}) async-done(((bf16[512,768]{1,0:T(8,128)(2,1)}, bf16[512,768]{1,0:T(8,128)(2,1)}), (bf16[512,768]{1,0:T(8,128)(2,1)}, bf16[512,768]{1,0:T(8,128)(2,1)})) %all-reduce.31.cloned.1.call-update) | async-done | bytes 1572880 | tf_op jit(solution)/shard_map/psum | solution.py:154
  357.6 11.0 all-gather.10.cloned.1.call-done
  374.6 73.8 %all-gather.8.cloned.1.call-done = bf16[4,768,768]{2,1,0:T(8,128)(2,1)} async-done(((bf16[4,96,768]{2,1,0:T(8,128)(2,1)}), bf16[4,768,768]{2,1,0:T(8,128)(2,1)}) %all-gather.8.cloned.1.call-update) | async-done | bytes 4718608 | tf_op jit(solution)/shard_map/all_gather | solution.py:116
  448.4 7.4 fusion.12
  458.9 8.4 scatter_custom_fusion.2
  468.3 6.5 fusion.138
  474.8 9.7 scatter_custom_fusion
  498.6 8.4 scatter_custom_fusion.3
  514.5 8.5 scatter_custom_fusion.1
  524.1 67.3 %all-reduce.29.cloned.1.call-done = (bf16[512,768]{1,0:T(8,128)(2,1)}, bf16[512,768]{1,0:T(8,128)(2,1)}, bf16[512,768]{1,0:T(8,128)(2,1)}, bf16[512,768]{1,0:T(8,128)(2,1)}) async-done(((bf16[512,768]{1,0:T(8,128)(2,1)}, bf16[512,768]{1,0:T(8,128)(2,1)}, bf16[512,768]{1,0:T(8,128)(2,1)}, bf16[512,768]{1,0:T(8,128)(2,1)}), (bf16[512,768]{1,0:T(8,128)(2,1)}, bf16[512,768]{1,0:T(8,128)(2,1)}, ...) | async-done | bytes 3145744 | tf_op jit(solution)/shard_map/psum | solution.py:272
  684.5 48.2 %rev.23 = f32[3,512,1024]{2,1,0:T(8,128)} reverse(bf16[3,512,1024]{2,1,0:T(8,128)(2,1)} %copy-done.4), dimensions={2} | reverse | bytes 9437184 | tf_op jit(solution)/shard_map/rev | solution.py:42
  732.7 48.1 %rev.22 = f32[3,512,1024]{2,1,0:T(8,128)} reverse(bf16[3,512,1024]{2,1,0:T(8,128)(2,1)} %copy-done.3), dimensions={2} | reverse | bytes 9437184 | tf_op jit(solution)/shard_map/rev | solution.py:42
  785.1 19.9 %copy.87 = f32[1,3,512,1536]{3,1,2,0:T(4,128)S(1)} copy(f32[1,3,512,1536]{3,2,1,0:T(8,128)S(1)} %pad_bitcast_fusion) | data formatting | bytes 18874368
  810.8 13.2 %reshape.680 = f32[2357760]{0:T(1024)} reshape(f32[3,785920]{1,0:T(4,128)} %slice.158) | data formatting | bytes 18862080
  824.0 15.8 %reshape.559 = f32[3,512,1535]{2,1,0:T(8,128)} reshape(f32[2357760]{0:T(1024)} %reshape.680) | data formatting | bytes 18862080 | tf_op jit(solution)/shard_map/reshape | solution.py:46
  848.3 19.9 %copy.86 = f32[1,3,512,1536]{3,1,2,0:T(4,128)S(1)} copy(f32[1,3,512,1536]{3,2,1,0:T(8,128)S(1)} %pad_bitcast_fusion.1) | data formatting | bytes 18874368
  874.2 13.3 %reshape.678 = f32[2357760]{0:T(1024)} reshape(f32[3,785920]{1,0:T(4,128)} %slice.157) | data formatting | bytes 18862080
  887.5 15.9 %reshape.557 = f32[3,512,1535]{2,1,0:T(8,128)} reshape(f32[2357760]{0:T(1024)} %reshape.678) | data formatting | bytes 18862080 | tf_op jit(solution)/shard_map/reshape | solution.py:46
  917.4 38.1 %all-reduce.18 = (f32[768]{0:T(1024)S(1)}, f32[32,3]{0,1:T(4,128)}, f32[768]{0:T(1024)S(1)}) all-reduce(f32[768]{0:T(1024)S(1)} %add.402, f32[32,3]{0,1:T(4,128)S(1)} %fusion.78, f32[768]{0:T(1024)S(1)} %add.409), channel_id=8, replica_groups=mesh['dp'=4,'ctx'=2,'tensor'=4] {'dp','ctx'}, use_global_device_ids=true, to_apply=%region_42.43.clone | all-reduce | flops 1632 | bytes 13056
  962.8 95.3 %reduce-scatter.20.cloned.1.call-done = f32[4,768,96]{1,2,0:T(8,128)} async-done(((f32[4,768,768]{1,2,0:T(8,128)}), f32[4,768,96]{1,2,0:T(8,128)}) %reduce-scatter.20.cloned.1.call-update) | async-done | bytes 1179664 | tf_op jit(solution)/shard_map/reduce_scatter | solution.py:391
  1058.0 166.4 %reduce-scatter.18.cloned.1.call-done = f32[4,96,768]{2,1,0:T(8,128)} async-done(((f32[4,768,768]{2,1,0:T(8,128)}), f32[4,96,768]{2,1,0:T(8,128)}) %reduce-scatter.18.cloned.1.call-update) | async-done | bytes 1179664 | tf_op jit(solution)/shard_map/reduce_scatter | solution.py:390
  (345 shorter events, 260.9 us)
Async XLA Ops:
  8.0 130.7 %copy-start = (f32[32,3]{0,1:T(4,128)S(1)}, f32[32,3]{0,1:T(4,128)}, u32[]{:S(2)}) copy-start(f32[32,3]{0,1:T(4,128)} %param.26) | copy-start | bytes 1156
  8.0 34.0 %copy-start.59 = (bf16[3,96,192]{2,1,0:T(8,128)(2,1)S(1)}, bf16[3,96,192]{2,1,0:T(8,128)(2,1)}, u32[]{:S(2)}) copy-start(bf16[3,96,192]{2,1,0:T(8,128)(2,1)} %param.24) | copy-start | bytes 331780
  8.0 321.5 %all-reduce.31.cloned.1.call-start = ((), (), s32[]{:S(2)}) async-start(), calls=%async_computation.18 | async-start | bytes 3145728 | tf_op jit(solution)/shard_map/psum | solution.py:154
  39.8 69.5 %copy-start.61 = (f32[512]{0:T(512)}, f32[512]{0:T(512)S(1)}, u32[]{:S(2)}) copy-start(f32[512]{0:T(512)S(1)} %fusion.121) | copy-start | bytes 6148
  73.2 212.3 %copy-start.22 = (bf16[192,768]{0,1:T(8,128)(2,1)}, bf16[192,768]{0,1:T(8,128)(2,1)S(1)}, u32[]{:S(2)}) copy-start(bf16[192,768]{0,1:T(8,128)(2,1)S(1)} %all_gather.26) | copy-start | bytes 884740
  73.2 36.0 %copy-start.2 = (bf16[2,512,768]{2,1,0:T(8,128)(2,1)S(1)}, bf16[2,512,768]{2,1,0:T(8,128)(2,1)}, u32[]{:S(2)}) copy-start(bf16[2,512,768]{2,1,0:T(8,128)(2,1)} %param.19) | copy-start | bytes 4718596
  118.6 136.2 %copy-start.32 = (bf16[1,1024,192]{1,2,0:T(8,128)(2,1)}, bf16[1,1024,192]{1,2,0:T(8,128)(2,1)S(1)}, u32[]{:S(2)}) copy-start(bf16[1,1024,192]{1,2,0:T(8,128)(2,1)S(1)} %all-gather.2) | copy-start | bytes 1179652
  125.9 133.8 %copy-start.40 = (bf16[1,512,192]{1,2,0:T(8,128)(2,1)}, bf16[1,512,192]{1,2,0:T(8,128)(2,1)S(1)}, u32[]{:S(2)}) copy-start(bf16[1,512,192]{1,2,0:T(8,128)(2,1)S(1)} %get-tuple-element.100) | copy-start | bytes 589828
  132.2 127.4 %copy-start.34 = (bf16[1,1024,192]{1,2,0:T(8,128)(2,1)}, bf16[1,1024,192]{1,2,0:T(8,128)(2,1)S(1)}, u32[]{:S(2)}) copy-start(bf16[1,1024,192]{1,2,0:T(8,128)(2,1)S(1)} %all-gather) | copy-start | bytes 1179652
  201.7 52.3 %copy-start.69 = (s32[512]{0:T(512)S(1)}, s32[512]{0:T(512)}, u32[]{:S(2)}) copy-start(s32[512]{0:T(512)} %iota_add_fusion) | copy-start | bytes 6148
  254.7 23.6 %copy-start.30 = (pred[512,1024]{1,0:T(8,128)(4,1)}, pred[512,1024]{1,0:T(8,128)(4,1)S(1)}, u32[]{:S(2)}) copy-start(pred[512,1024]{1,0:T(8,128)(4,1)S(1)} %get-tuple-element.112) | copy-start | bytes 1572868
  254.7 26.6 %copy-start.28 = (pred[512,1024]{1,0:T(8,128)(4,1)}, pred[512,1024]{1,0:T(8,128)(4,1)S(1)}, u32[]{:S(2)}) copy-start(pred[512,1024]{1,0:T(8,128)(4,1)S(1)} %get-tuple-element.111) | copy-start | bytes 1572868
  259.6 21.7 %copy-start.5 = (f32[3,512,1024]{2,1,0:T(8,128)}, f32[3,512,1024]{2,1,0:T(8,128)S(1)}, u32[]{:S(2)}) copy-start(f32[3,512,1024]{2,1,0:T(8,128)S(1)} %get-tuple-element.122) | copy-start | bytes 18874372
  261.6 16.7 %copy-start.6 = (f32[3,512,1024]{2,1,0:T(8,128)}, f32[3,512,1024]{2,1,0:T(8,128)S(1)}, u32[]{:S(2)}) copy-start(f32[3,512,1024]{2,1,0:T(8,128)S(1)} %get-tuple-element.118) | copy-start | bytes 18874372
  285.5 21.9 %copy-start.60 = (s32[2,1,4,256]{3,2,1,0:T(4,128)S(1)}, s32[2,1,4,256]{3,2,1,0:T(4,128)}, u32[]{:S(2)}) copy-start(s32[2,1,4,256]{3,2,1,0:T(4,128)} %param.22) | copy-start | bytes 24580
  286.8 21.9 %copy-start.72 = (s32[2,512]{1,0:T(2,128)S(1)}, s32[2,512]{1,0:T(2,128)}, u32[]{:S(2)}) copy-start(s32[2,512]{1,0:T(2,128)} %param.21) | copy-start | bytes 12292
  286.9 81.7 %all-gather.10.cloned.1.call-start = ((), (), s32[]{:S(2)}) async-start(), calls=%async_computation.8 | async-start | bytes 5308416 | tf_op jit(solution)/shard_map/all_gather | solution.py:117
  287.4 160.9 %all-gather.8.cloned.1.call-start = ((), (), s32[]{:S(2)}) async-start(), calls=%async_computation.7 | async-start | bytes 5308416 | tf_op jit(solution)/shard_map/all_gather | solution.py:116
  288.0 303.4 %all-reduce.29.cloned.1.call-start = ((), (), s32[]{:S(2)}) async-start(), calls=%async_computation.17 | async-start | bytes 6291456 | tf_op jit(solution)/shard_map/psum | solution.py:272
  368.6 79.8 %copy-start.21 = (bf16[1024,768]{1,0:T(8,128)(2,1)S(1)}, bf16[1024,768]{1,0:T(8,128)(2,1)}, u32[]{:S(2)}) copy-start(bf16[1024,768]{1,0:T(8,128)(2,1)} %gather_fusion) | copy-start | bytes 4718596
  524.0 67.4 %copy-start.12 = (bf16[2,512,768]{2,1,0:T(8,128)(2,1)S(1)}, bf16[2,512,768]{2,1,0:T(8,128)(2,1)}, u32[]{:S(2)}) copy-start(bf16[2,512,768]{2,1,0:T(8,128)(2,1)} %param.31) | copy-start | bytes 4718596
  524.0 118.3 %reduce-scatter.14.cloned.1.call-start = ((), (), s32[]{:S(2)}) async-start(), calls=%async_computation.9 | async-start | bytes 1179648 | tf_op jit(solution)/shard_map/reduce_scatter | solution.py:344
  609.2 37.3 %reduce-scatter.16.cloned.1.call-start = ((), (), s32[]{:S(2)}) async-start(), calls=%async_computation.10 | async-start | bytes 1179648 | tf_op jit(solution)/shard_map/reduce_scatter | solution.py:344
  622.6 288.8 %reduce-scatter.26.cloned.1.call-start = ((), (), s32[]{:S(2)}) async-start(), calls=%async_computation.15 | async-start | bytes 442368
  633.5 279.4 %reduce-scatter.24.cloned.1.call-start = ((), (), s32[]{:S(2)}) async-start(), calls=%async_computation.14 | async-start | bytes 884736
  638.6 275.8 %all-reduce.27.cloned.1.call-start = ((), (), s32[]{:S(2)}) async-start(), calls=%async_computation.16 | async-start | bytes 3145728 | tf_op jit(solution)/shard_map/psum | solution.py:357
  652.6 308.3 %reduce-scatter.22.cloned.1.call-start = ((), (), s32[]{:S(2)}) async-start(), calls=%async_computation.13 | async-start | bytes 2211840
  665.5 392.5 %reduce-scatter.20.cloned.1.call-start = ((), (), s32[]{:S(2)}) async-start(), calls=%async_computation.12 | async-start | bytes 10616832 | tf_op jit(solution)/shard_map/reduce_scatter | solution.py:391
  675.0 549.5 %reduce-scatter.18.cloned.1.call-start = ((), (), s32[]{:S(2)}) async-start(), calls=%async_computation.11 | async-start | bytes 10616832 | tf_op jit(solution)/shard_map/reduce_scatter | solution.py:390
  911.3 45.4 %copy-start.66 = (f32[512]{0:T(512)S(1)}, f32[512]{0:T(512)}, u32[]{:S(2)}) copy-start(f32[512]{0:T(512)} %copy-done.65) | copy-start | bytes 6148
  911.4 45.4 %copy-start.64 = (f32[512]{0:T(512)S(1)}, f32[512]{0:T(512)}, u32[]{:S(2)}) copy-start(f32[512]{0:T(512)} %copy-done.63) | copy-start | bytes 6148
  959.6 264.9 %copy-start.1 = (f32[32,3]{0,1:T(4,128)S(1)}, f32[32,3]{0,1:T(4,128)}, u32[]{:S(2)}) copy-start(f32[32,3]{0,1:T(4,128)} %param.26) | copy-start | bytes 1156
  (61 other events, 213.8 us)
Sparse Core Ops, SparseCore 0:
  287.0 42.5 all-reduce.30
  524.2 67.2 all-reduce.28
  609.3 17.4 reduce-scatter.13
  629.1 17.4 reduce-scatter.15
  649.7 61.5 reduce-scatter.25
  714.4 61.5 reduce-scatter.23
  778.6 41.9 all-reduce.26
  824.5 66.7 reduce-scatter.21
  895.4 162.5 reduce-scatter.19
  1062.1 162.3 reduce-scatter.17
Sparse Core Ops, SparseCore 1:
  289.5 79.0 all-gather.9
  370.6 77.7 all-gather.7
where the time goes:
time: 1250 us; the launch traced here: 1230 us
  waiting for transfers between devices  438 us (35%)
  local copies, waits for them, and re-layouts  390 us (31%)
  blocking collectives  173 us (14%)
  matrix products  120 us (10%)
  other arithmetic  92.6 us (7%)
  between operations  18.6 us (1%)
    reduce_scatter x1, waiting for transfers between devices, body(): lax.psum_scatter(grad_sums[5], ('dp', 'ctx'), scatter_dimension=1, tiled=...  166 us
    unnamed x194, local copies, waits for them, and re-layouts  136 us
    rev x2, local copies, waits for them, and re-layouts, diagonal_sums(): flipped = jnp.pad(gradient[:, :, ::-1], ((0, 0), (0, 0), (0, query_count)))  96.3 us
    reduce_scatter x1, waiting for transfers between devices, body(): lax.psum_scatter(grad_sums[6], ('dp', 'ctx'), scatter_dimension=2, tiled=...  95.3 us
    all_gather x1, waiting for transfers between devices, body(): lax.all_gather(up_weight, ('dp', 'ctx'), axis=1, tiled=True)  73.8 us
    psum x1, waiting for transfers between devices, body(): lax.psum(spread_grad.astype(jnp.bfloat16), 'tensor').astype(jnp.float32)  67.3 us
    unnamed x2, blocking collectives  61.8 us
    rev x1, local copies, waits for them, and re-layouts, toeplitz(): return repeated[:, :, ::-1]  51 us
  transfers between devices with their start and end apart: 12, of which 7 were waited for; matrix products, arithmetic and copies ran while one was open for 28% of the time, Pallas kernels for 0%

commit v1 on v0

--- a/solution.py
+++ b/solution.py
@@ -1,13 +1,743 @@
+import functools
+
 import jax
 import jax.numpy as jnp
 import numpy as np
 from jax import lax
+from jax.experimental import pallas as pl
+from jax.experimental.pallas import tpu as pltpu
 from jax.sharding import PartitionSpec as P
 
 BUCKETS = 32
+MESH = pl.DeviceIdType.MESH
+BF = jnp.bfloat16
+F32 = jnp.float32
 
 
 bucket_edges = np.ceil(16.0 * 8.0 ** (np.arange(1, 16) / 16.0)).astype(np.int32)
+bucket_starts = [int(n) for n in range(17)] + [int(n) for n in bucket_edges]
+
+
+QT = 256
+BAND = 128
+
+
+def mm(a, b):
+    return jnp.dot(a, b, preferred_element_type=F32)
+
+
+def mm_nt(a, b):
+    return lax.dot_general(a, b, (((1,), (1,)), ((), ())), preferred_element_type=F32)
+
+
+def mm_tn(a, b):
+    return lax.dot_general(a, b, (((0,), (0,)), ((), ())), preferred_element_type=F32)
+
+
+class Group:
+    def __init__(self, place, src, dst_at, zs, zr, xs, xr, local):
+        self.dp, self.cx, self.t = place
+        self.src, self.dst_at = src, dst_at
+        self.zs, self.zr, self.xs, self.xr, self.local = zs, zr, xs, xr, local
+
+    def slab(self, k, cx):
+        return lax.rem(self.dp + 4 - k, 4) * 2 + cx
+
+    def own(self):
+        return pltpu.make_async_copy(self.src, self.dst_at(self.slab(0, self.cx)), self.local)
+
+    def z_send(self, k):
+        return pltpu.make_async_remote_copy(
+            src_ref=self.src,
+            dst_ref=self.dst_at(self.slab(0, self.cx)),
+            send_sem=self.zs(k - 1),
+            recv_sem=self.zr(k - 1),
+            device_id=(lax.rem(self.dp + k, 4), self.cx, self.t),
+            device_id_type=MESH,
+        )
+
+    def z_recv(self, k):
+        return pltpu.make_async_remote_copy(
+            src_ref=self.src,
+            dst_ref=self.dst_at(self.slab(k, self.cx)),
+            send_sem=self.zs(k - 1),
+            recv_sem=self.zr(k - 1),
+            device_id=(lax.rem(self.dp + k, 4), self.cx, self.t),
+            device_id_type=MESH,
+        )
+
+    def x_send(self, k):
+        spot = self.dst_at(self.slab(k, self.cx))
+        return pltpu.make_async_remote_copy(
+            src_ref=self.src if k == 0 else spot,
+            dst_ref=spot,
+            send_sem=self.xs(k),
+            recv_sem=self.xr(k),
+            device_id=(self.dp, 1 - self.cx, self.t),
+            device_id_type=MESH,
+        )
+
+    def x_recv(self, k):
+        spot = self.dst_at(self.slab(k, 1 - self.cx))
+        return pltpu.make_async_remote_copy(
+            src_ref=self.src,
+            dst_ref=spot,
+            send_sem=self.xs(k),
+            recv_sem=self.xr(k),
+            device_id=(self.dp, 1 - self.cx, self.t),
+            device_id_type=MESH,
+        )
+
+    def begin(self):
+        self.own().start()
+        for k in (1, 3, 2):
+            self.z_send(k).start()
+        self.x_send(0).start()
+
+    def hand_on(self):
+        for k in (1, 3, 2):
+            self.z_recv(k).wait_recv()
+            self.x_send(k).start()
+
+    def finish(self):
+        self.own().wait()
+        for k in range(4):
+            self.x_recv(k).wait_recv()
+
+    def drain(self):
+        for k in (1, 2, 3):
+            self.z_send(k).wait_send()
+        for k in range(4):
+            self.x_send(k).wait_send()
+
+
+def lane_halves(shape):
+    return lax.broadcasted_iota(jnp.int32, shape, len(shape) - 1) < 64
+
+
+def head_cut(h):
+    return (h // 2) * 128, h % 2 == 0
+
+
+def head_tile(block, h, heads):
+    if block.shape[-1] == 64:
+        return block
+    lower = lane_halves(block.shape)
+    keep = lower if h % 2 == 0 else jnp.logical_not(lower)
+    return jnp.where(keep, block, jnp.zeros_like(block))
+
+
+def lanes_of(h, heads):
+    first = (h // 2) * 128
+    return slice(first, min(first + 128, heads * 64))
+
+
+def fill_bias(bias_ref, band_ref, heads):
+    rows = lax.broadcasted_iota(jnp.int32, (BAND, 2 * BAND), 0)
+    cols = lax.broadcasted_iota(jnp.int32, (BAND, 2 * BAND), 1)
+    away = rows + BAND - cols
+    for h in range(heads):
+        tile = jnp.full((BAND, 2 * BAND), bias_ref[0, h], F32)
+        for b in range(1, BUCKETS):
+            tile = jnp.where(away >= bucket_starts[b], bias_ref[b, h], tile)
+        band_ref[h] = tile - bias_ref[BUCKETS - 1, h]
+
+
+def masked_scores(q_tile, keys, band_ref, scores, h, first, length):
+    count = keys.shape[0]
+    scores[:, BAND:] = mm_nt(q_tile, keys) * 0.125
+    for part in range(QT // BAND):
+        spot = (
+            pl.ds(part * BAND, BAND),
+            pl.ds(pl.multiple_of(first + part * BAND, BAND), 2 * BAND),
+        )
+        scores[spot] = scores[spot] + band_ref[h]
+    values = scores[:, BAND:]
+    key_pos = lax.broadcasted_iota(jnp.int32, (QT, count), 1)
+    query_pos = lax.broadcasted_iota(jnp.int32, (QT, count), 0) + first
+    allowed = (key_pos <= query_pos) & (key_pos < length)
+    return jnp.where(allowed, values, -1e30), allowed
+
+
+def first_kernel(
+    heads,
+    len_ref,
+    bias_ref,
+    tok,
+    small,
+    wqkv,
+    wo,
+    w,
+    hidden,
+    ntwo,
+    normed,
+    q,
+    kcat,
+    vcat,
+    lse,
+    ab,
+    wqkv_full,
+    wo_own,
+    gains,
+    w_full,
+    small_all,
+    wo_full,
+    ab_all,
+    band,
+    scores,
+    sm_s,
+    sm_r,
+    q_s,
+    q_r,
+    o_s,
+    o_r,
+    ot_s,
+    ot_r,
+    kv_s,
+    kv_r,
+    ab_s,
+    ab_r,
+    w_s,
+    w_r,
+    local,
+):
+    dp, cx, t = lax.axis_index("dp"), lax.axis_index("ctx"), lax.axis_index("tensor")
+    place = (dp, cx, t)
+    seg = tok.shape[0] // 2
+    experts = w.shape[0]
+    group_peers = [
+        (lax.rem(dp + k, 4), cx if c == 0 else 1 - cx, t)
+        for k in range(4)
+        for c in range(2)
+        if (k, c) != (0, 0)
+    ]
+    group_from = [
+        lax.rem(dp + 4 - k, 4) * 2 + (cx if c == 0 else 1 - cx)
+        for k in range(4)
+        for c in range(2)
+        if (k, c) != (0, 0)
+    ]
+    tensor_peers = [(dp, cx, lax.rem(t + k, 4)) for k in (1, 2, 3)]
+    own_slab = dp * 2 + cx
+
+    barrier = pltpu.get_barrier_semaphore()
+    for peer in group_peers + tensor_peers:
+        pl.semaphore_signal(barrier, inc=1, device_id=peer, device_id_type=MESH)
+    pl.semaphore_wait(barrier, len(group_peers) + len(tensor_peers))
+
+    def small_send(i):
+        return pltpu.make_async_remote_copy(
+            src_ref=small,
+            dst_ref=small_all.at[own_slab],
+            send_sem=sm_s.at[i],
+            recv_sem=sm_r.at[i],
+            device_id=group_peers[i],
+            device_id_type=MESH,
+        )
+
+    def small_recv(i):
+        return pltpu.make_async_remote_copy(
+            src_ref=small,
+            dst_ref=small_all.at[group_from[i]],
+            send_sem=sm_s.at[i],
+            recv_sem=sm_r.at[i],
+            device_id=group_peers[i],
+            device_id_type=MESH,
+        )
+
+    small_own = pltpu.make_async_copy(small, small_all.at[own_slab], local.at[0])
+
+    def rows96(s):
+        return pl.ds(pl.multiple_of(s * 96, 32), 96)
+
+    g_qkv = Group(
+        place,
+        wqkv,
+        lambda s: wqkv_full.at[:, rows96(s), :],
+        lambda i: q_s.at[i],
+        lambda i: q_r.at[i],
+        lambda i: q_s.at[3 + i],
+        lambda i: q_r.at[3 + i],
+        local.at[1],
+    )
+    g_out = Group(
+        place,
+        wo,
+        lambda s: wo_full.at[t, rows96(s), :],
+        lambda i: o_s.at[i],
+        lambda i: o_r.at[i],
+        lambda i: o_s.at[3 + i],
+        lambda i: o_r.at[3 + i],
+        local.at[2],
+    )
+    g_w = [
+        Group(
+            place,
+            w.at[e],
+            lambda s, e=e: w_full.at[e, :, rows96(s), :],
+            lambda i, e=e: w_s.at[e, i],
+            lambda i, e=e: w_r.at[e, i],
+            lambda i, e=e: w_s.at[e, 3 + i],
+            lambda i, e=e: w_r.at[e, 3 + i],
+            local.at[3 + e],
+        )
+        for e in range(experts)
+    ]
+
+    small_own.start()
+    for i in range(7):
+        small_send(i).start()
+    g_qkv.begin()
+    g_out.begin()
+
+    @pl.when(cx == 0)
+    def _():
+        for m in range(2):
+            kcat[m, seg:, :] = jnp.zeros((seg, kcat.shape[2]), BF)
+            vcat[m, seg:, :] = jnp.zeros((seg, kcat.shape[2]), BF)
+
+    fill_bias(bias_ref, band, heads)
+
+    small_own.wait()
+    for i in range(7):
+        small_recv(i).wait_recv()
+    total = small_all[0].astype(F32)
+    for i in range(1, 8):
+        total = total + small_all[i].astype(F32)
+    gains[...] = total
+
+    def norm_rows(i, carry):
+        rows = pl.ds(pl.multiple_of(i * 128, 128), 128)
+        x = tok[rows, :].astype(F32)
+        scale = lax.rsqrt(jnp.mean(x * x, axis=-1, keepdims=True) + 1e-06)
+        normed[rows, :] = (x * scale * gains[0:1, :]).astype(BF)
+        return carry
+
+    lax.fori_loop(0, 2 * seg // 128, norm_rows, 0)
+
+    g_qkv.hand_on()
+    for e in range(experts):
+        g_w[e].begin()
+    g_out.hand_on()
+    g_qkv.finish()
+
+    def project(m):
+        def step(i, carry):
+            rows = pl.ds(pl.multiple_of(m * seg + i * 256, 256), 256)
+            spots = pl.ds(pl.multiple_of(cx * seg + i * 256, 256), 256)
+            x = normed[rows, :]
+            q[rows, :] = mm(x, wqkv_full[0]).astype(BF)
+            kcat[m, spots, :] = mm(x, wqkv_full[1]).astype(BF)
+            vcat[m, spots, :] = mm(x, wqkv_full[2]).astype(BF)
+            return carry
+
+        lax.fori_loop(0, seg // 256, step, 0)
+
+    def kv_copy(m, which):
+        ref = (kcat, vcat)[which]
+        return pltpu.make_async_remote_copy(
+            src_ref=ref.at[m, pl.ds(0, seg), :],
+            dst_ref=ref.at[m, pl.ds(0, seg), :],
+            send_sem=kv_s.at[m * 2 + which],
+            recv_sem=kv_r.at[m * 2 + which],
+            device_id=(dp, 1 - cx, t),
+            device_id_type=MESH,
+        )
+
+    for m in range(2):
+        project(m)
+
+        @pl.when(cx == 0)
+        def _():
+            kv_copy(m, 0).start()
+            kv_copy(m, 1).start()
+
+    g_out.finish()
+
+    def wo_send(k):
+        return pltpu.make_async_remote_copy(
+            src_ref=wo_full.at[t],
+            dst_ref=wo_full.at[t],
+            send_sem=ot_s.at[k - 1],
+            recv_sem=ot_r.at[k - 1],
+            device_id=tensor_peers[k - 1],
+            device_id_type=MESH,
+        )
+
+    def wo_recv(k):
+        spot = wo_full.at[lax.rem(t + 4 - k, 4)]
+        return pltpu.make_async_remote_copy(
+            src_ref=spot,
+            dst_ref=spot,
+            send_sem=ot_s.at[k - 1],
+            recv_sem=ot_r.at[k - 1],
+            device_id=tensor_peers[k - 1],
+            device_id_type=MESH,
+        )
+
+    for k in (1, 2, 3):
+        wo_send(k).start()
+
+    def ab_copy(m, k, source):
+        spot = ab_all.at[source, pl.ds(m * seg, seg), :]
+        return pltpu.make_async_remote_copy(
+            src_ref=spot,
+            dst_ref=spot,
+            send_sem=ab_s.at[m * 3 + k - 1],
+            recv_sem=ab_r.at[m * 3 + k - 1],
+            device_id=tensor_peers[k - 1],
+            device_id_type=MESH,
+        )
+
+    def attend(m):
+        length = len_ref[m]
+
+        def step(i, carry):
+            rows = pl.ds(pl.multiple_of(m * seg + i * QT, QT), QT)
+            first = cx * seg + i * QT
+            lanes128 = lax.broadcasted_iota(jnp.int32, (QT, 128), 1)
+            tops = jnp.zeros((QT, 128), F32)
+            held = []
+            for h in range(heads):
+                cut = lanes_of(h, heads)
+                q_tile = head_tile(q[rows, cut], h, heads)
+                values, allowed = masked_scores(
+                    q_tile, kcat[m, :, cut], band, scores, h, first, length
+                )
+                top = jnp.max(values, axis=-1, keepdims=True)
+                raised = jnp.where(allowed, jnp.exp(values - top), 0.0)
+                mass = jnp.sum(raised, axis=-1, keepdims=True)
+                probs = (raised * (1.0 / mass)).astype(BF)
+                held.append(mm(probs, vcat[m, :, cut]))
+                tops = jnp.where(lanes128 == h, top + jnp.log(mass), tops)
+                if h % 2 == 1:
+                    both = jnp.where(lane_halves(held[0].shape), held[0], held[1])
+                    ab_all[t, rows, cut] = both.astype(BF)
+                    held = []
+                elif h == heads - 1:
+                    ab_all[t, rows, cut] = held[0].astype(BF)
+            lse[rows, :] = tops
+            return carry
+
+        lax.fori_loop(0, seg // QT, step, 0)
+
+    for m in range(2):
+
+        @pl.when(cx == 1)
+        def _():
+            kv_copy(m, 0).wait_recv()
+            kv_copy(m, 1).wait_recv()
+
+        attend(m)
+        for k in (1, 2, 3):
+            ab_copy(m, k, t).start()
+        if m == 0:
+            g_w[0].hand_on()
+    for k in (1, 2, 3):
+        wo_recv(k).wait_recv()
+    wo_own[...] = wo_full[t]
+    ab[...] = ab_all[t]
+
+    for m in range(2):
+        for k in (1, 2, 3):
+            ab_copy(m, k, lax.rem(t + 4 - k, 4)).wait_recv()
+
+        def branch(i, carry):
+            rows = pl.ds(pl.multiple_of(m * seg + i * 256, 256), 256)
+            total = mm_nt(ab_all[0, rows, :], wo_full[0])
+            for j in range(1, 4):
+                total = total + mm_nt(ab_all[j, rows, :], wo_full[j])
+            x = tok[rows, :].astype(F32) + total
+            hidden[rows, :] = x
+            scale = lax.rsqrt(jnp.mean(x * x, axis=-1, keepdims=True) + 1e-06)
+            ntwo[rows, :] = (x * scale * gains[1:2, :]).astype(BF)
+            return carry
+
+        lax.fori_loop(0, seg // 256, branch, 0)
+        if m == 0 and experts > 1:
+            g_w[1].hand_on()
+
+    for e in range(2, experts):
+        g_w[e].hand_on()
+    for e in range(experts):
+        g_w[e].finish()
+
+    for i in range(7):
+        small_send(i).wait_send()
+    g_qkv.drain()
+    g_out.drain()
+    for e in range(experts):
+        g_w[e].drain()
+    for k in (1, 2, 3):
+        wo_send(k).wait_send()
+    for m in range(2):
+        for k in (1, 2, 3):
+            ab_copy(m, k, t).wait_send()
+
+        @pl.when(cx == 0)
+        def _():
+            kv_copy(m, 0).wait_send()
+            kv_copy(m, 1).wait_send()
+
+
+def first_call(lengths, bias, tok, small, wqkv, wo, w):
+    heads = bias.shape[1]
+    rows, width = tok.shape
+    span = wqkv.shape[2]
+    experts = w.shape[0]
+    ff = w.shape[3]
+    vm = pl.BlockSpec(memory_space=pltpu.VMEM)
+    sm = pl.BlockSpec(memory_space=pltpu.SMEM)
+    hbm = pl.BlockSpec(memory_space=pl.ANY)
+    dma = pltpu.SemaphoreType.DMA
+    return pl.pallas_call(
+        functools.partial(first_kernel, heads),
+        out_shape=(
+            jax.ShapeDtypeStruct((rows, width), F32),
+            jax.ShapeDtypeStruct((rows, width), BF),
+            jax.ShapeDtypeStruct((rows, width), BF),
+            jax.ShapeDtypeStruct((rows, span), BF),
+            jax.ShapeDtypeStruct((2, rows, span), BF),
+            jax.ShapeDtypeStruct((2, rows, span), BF),
+            jax.ShapeDtypeStruct((rows, 128), F32),
+            jax.ShapeDtypeStruct((rows, span), BF),
+            jax.ShapeDtypeStruct((3, width, span), BF),
+            jax.ShapeDtypeStruct((width, span), BF),
+            jax.ShapeDtypeStruct((16, width), F32),
+            jax.ShapeDtypeStruct((experts, 2, width, ff), BF),
+        ),
+        in_specs=[sm, sm, vm, hbm, hbm, hbm, hbm],
+        out_specs=(vm,) * 11 + (hbm,),
+        scratch_shapes=[
+            pltpu.VMEM((8, 16, width), BF),
+            pltpu.VMEM((4, width, span), BF),
+            pltpu.VMEM((4, rows, span), BF),
+            pltpu.VMEM((heads, BAND, 2 * BAND), F32),
+            pltpu.VMEM((QT, rows + BAND), F32),
+            dma((7,)),
+            dma((7,)),
+            dma((7,)),
+            dma((7,)),
+            dma((7,)),
+            dma((7,)),
+            dma((3,)),
+            dma((3,)),
+            dma((4,)),
+            dma((4,)),
+            dma((6,)),
+            dma((6,)),
+            dma((experts, 7)),
+            dma((experts, 7)),
+            dma((3 + experts,)),
+        ],
+        compiler_params=pltpu.CompilerParams(
+            collective_id=0, has_side_effects=True, vmem_limit_bytes=56 << 20
+        ),
+    )(lengths, bias, tok, small, wqkv, wo, w)
+
+
+def back_kernel(heads, len_ref, bias_ref, q, kcat, vcat, lse, grad, dq, dk, dv, dbias, band, scores, spread, band_sum, whole_sum):
+    cx = lax.axis_index("ctx")
+    seg = q.shape[0] // 2
+    fill_bias(bias_ref, band, heads)
+    dk[...] = jnp.zeros(dk.shape, F32)
+    dv[...] = jnp.zeros(dv.shape, F32)
+    spread[...] = jnp.zeros(spread.shape, F32)
+    band_sum[...] = jnp.zeros(band_sum.shape, F32)
+    whole_sum[...] = jnp.zeros(whole_sum.shape, F32)
+    for m in range(2):
+        length = len_ref[m]
+
+        def step(i, carry):
+            rows = pl.ds(pl.multiple_of(m * seg + i * QT, QT), QT)
+            first = cx * seg + i * QT
+            held = []
+            for h in range(heads):
+                cut = lanes_of(h, heads)
+                q_tile = head_tile(q[rows, cut], h, heads)
+                do_tile = head_tile(grad[rows, cut], h, heads)
+                values, allowed = masked_scores(
+                    q_tile, kcat[m, :, cut], band, scores, h, first, length
+                )
+                soft = jnp.where(allowed, jnp.exp(values - lse[rows, h : h + 1]), 0.0)
+                soft_grad = mm_nt(do_tile, vcat[m, :, cut])
+                dv[m, :, cut] += mm_tn(soft.astype(BF), do_tile)
+                delta = jnp.sum(soft * soft_grad, axis=-1, keepdims=True)
+                score_grad = (soft * (soft_grad - delta)).astype(BF)
+                dk[m, :, cut] += mm_tn(score_grad, q_tile)
+                held.append(mm(score_grad, kcat[m, :, cut]) * 0.125)
+                spread[:, BAND:] = score_grad.astype(F32)
+                for part in range(QT // BAND):
+                    lanes = pl.ds(pl.multiple_of(first + part * BAND, BAND), 2 * BAND)
+                    band_sum[h] += spread[part * BAND : (part + 1) * BAND, lanes]
+                whole_sum[h : h + 1, :] += jnp.sum(spread[:, BAND:], axis=0, keepdims=True)
+                if h % 2 == 1:
+                    both = jnp.where(lane_halves(held[0].shape), held[0], held[1])
+                    dq[rows, cut] = both.astype(BF)
+                    held = []
+                elif h == heads - 1:
+                    dq[rows, cut] = held[0].astype(BF)
+            return carry
+
+        lax.fori_loop(0, seg // QT, step, 0)
+    bucket_sums(heads, band_sum, whole_sum, dbias)
+
+
+def bucket_sums(heads, band_sum, whole_sum, dbias):
+    rows = lax.broadcasted_iota(jnp.int32, (BAND, 2 * BAND), 0)
+    cols = lax.broadcasted_iota(jnp.int32, (BAND, 2 * BAND), 1)
+    away = rows + BAND - cols
+    bucket = lax.broadcasted_iota(jnp.int32, (BUCKETS, 2 * BAND), 0)
+    lanes128 = lax.broadcasted_iota(jnp.int32, (BUCKETS, 128), 1)
+    result = jnp.zeros((BUCKETS, 128), F32)
+    for h in range(heads):
+        tile = band_sum[h]
+        sums = jnp.zeros((BUCKETS, 2 * BAND), F32)
+        for b in range(BUCKETS - 1):
+            inside = (away >= bucket_starts[b]) & (away < bucket_starts[b + 1])
+            row = jnp.sum(jnp.where(inside, tile, 0.0), axis=0, keepdims=True)
+            sums = jnp.where(bucket == b, row, sums)
+        per_bucket = jnp.sum(sums, axis=1, keepdims=True)
+        near = jnp.sum(per_bucket, axis=0, keepdims=True)
+        total = jnp.sum(whole_sum[h : h + 1, :], axis=1, keepdims=True)
+        last = lax.broadcasted_iota(jnp.int32, (BUCKETS, 1), 0) == BUCKETS - 1
+        per_bucket = jnp.where(last, total - near, per_bucket)
+        result = jnp.where(lanes128 == h, per_bucket, result)
+    dbias[...] = result
+
+
+def back_call(lengths, bias, q, kcat, vcat, lse, grad):
+    heads = bias.shape[1]
+    vm = pl.BlockSpec(memory_space=pltpu.VMEM)
+    sm = pl.BlockSpec(memory_space=pltpu.SMEM)
+    return pl.pallas_call(
+        functools.partial(back_kernel, heads),
+        out_shape=(
+            jax.ShapeDtypeStruct(q.shape, BF),
+            jax.ShapeDtypeStruct(kcat.shape, F32),
+            jax.ShapeDtypeStruct(kcat.shape, F32),
+            jax.ShapeDtypeStruct((BUCKETS, 128), F32),
+        ),
+        in_specs=[sm, sm] + [vm] * 5,
+        out_specs=(vm,) * 4,
+        scratch_shapes=[
+            pltpu.VMEM((heads, BAND, 2 * BAND), F32),
+            pltpu.VMEM((QT, q.shape[0] + BAND), F32),
+            pltpu.VMEM((QT, q.shape[0] + BAND), F32),
+            pltpu.VMEM((heads, BAND, 2 * BAND), F32),
+            pltpu.VMEM((8, q.shape[0]), F32),
+        ],
+        compiler_params=pltpu.CompilerParams(vmem_limit_bytes=56 << 20),
+    )(lengths, bias, q, kcat, vcat, lse, grad)
+
+
+def body_fast(
+    inputs, lengths, expert_ids, slot_rows, attn_gain, qkv_weight, out_weight, position_bias,
+    ffn_gain, router_weight, up_weight, down_weight, cotangent,
+):
+    micro, seg, width = inputs.shape
+    rows = micro * seg
+    experts = up_weight.shape[0]
+    cx = lax.axis_index("ctx")
+    slab = lax.axis_index("dp") * 2 + cx
+    shard = attn_gain.shape[0]
+    small_own = jnp.concatenate(
+        [attn_gain[None], ffn_gain[None], router_weight.T, jnp.zeros((10, shard), BF)], axis=0
+    )
+    small = lax.dynamic_update_slice(jnp.zeros((16, width), BF), small_own, (0, slab * shard))
+    w = jnp.stack([up_weight, jnp.transpose(down_weight, (0, 2, 1))], axis=1)
+    tok = inputs.reshape(rows, width)
+    (hidden, ntwo, normed, q, kcat, vcat, lse, ab, wqkv, wo, gains, w_full) = first_call(
+        lengths, position_bias, tok, small, qkv_weight, out_weight.T, w
+    )
+    gain_one, gain_two, router = gains[0], gains[1], gains[2 : 2 + experts].T.astype(BF)
+    f32dot = functools.partial(jnp.einsum, preferred_element_type=F32)
+    probs = jax.nn.softmax(f32dot("td,de->te", ntwo, router), axis=-1)
+    chosen = (expert_ids.reshape(rows)[:, None] == jnp.arange(experts)[None, :]).astype(F32)
+    gate = jnp.sum(probs * chosen, axis=-1)
+    positions = cx * seg + jnp.arange(seg, dtype=jnp.int32)
+    live = (positions[None, :] < lengths[:, None]).astype(F32).reshape(rows, 1)
+    upstream = live * cotangent.reshape(rows, width).astype(F32)
+    sum_grad = (gate[:, None] * upstream).astype(BF)
+    slots = slot_rows[:, 0]
+    place = jnp.where(slots < seg, slots + jnp.arange(micro)[:, None, None] * seg, rows)
+    place = jnp.transpose(place, (1, 0, 2)).reshape(experts, -1)
+    one_hot = (place[:, :, None] == jnp.arange(rows)[None, None, :]).astype(BF)
+    picked = f32dot("ekt,td->ekd", one_hot, ntwo).astype(BF)
+    slot_grad = f32dot("ekt,td->ekd", one_hot, sum_grad).astype(BF)
+    up, dn = w_full[:, 0], w_full[:, 1]
+    raised = f32dot("ekd,edf->ekf", picked, up)
+    activated, gelu_back = jax.vjp(jax.nn.gelu, raised)
+    activated = activated.astype(BF)
+    lowered = f32dot("ekf,edf->ekd", activated, dn).astype(BF)
+    spread = f32dot("ekt,ekd->td", one_hot, lowered).astype(BF)
+    down_part = f32dot("ekd,ekf->edf", slot_grad, activated)
+    act_grad = f32dot("ekd,edf->ekf", slot_grad, dn)
+    raised_grad = gelu_back(act_grad)[0].astype(BF)
+    up_part = f32dot("ekd,ekf->edf", picked, raised_grad)
+    picked_grad = f32dot("ekf,edf->ekd", raised_grad, up).astype(BF)
+    spread_grad = f32dot("ekt,ekd->td", one_hot, picked_grad).astype(BF)
+    expert_sum = lax.psum(spread, "tensor").astype(F32)
+    result = (live * (hidden + gate[:, None] * expert_sum)).astype(BF)
+    gate_grad = jnp.sum(expert_sum * upstream, axis=-1)
+    logit_grad = (probs * gate_grad[:, None] * (chosen - gate[:, None])).astype(BF)
+    router_part = f32dot("td,te->de", ntwo, logit_grad)
+    normed_two_grad = lax.psum(spread_grad, "tensor").astype(F32) + f32dot(
+        "te,de->td", logit_grad, router
+    )
+    unused, second_back = jax.vjp(rms_norm, hidden, gain_two)
+    hidden_grad, gain_two_part = second_back(normed_two_grad)
+    hidden_grad = hidden_grad + upstream
+    branch_grad = hidden_grad.astype(BF)
+    out_part = f32dot("td,te->de", branch_grad, ab)
+    attended_grad = f32dot("td,de->te", branch_grad, wo).astype(BF)
+    dq, dk, dv, dbias = back_call(lengths, position_bias, q, kcat, vcat, lse, attended_grad)
+    dkv = jnp.stack([dk * 0.125, dv], axis=0).astype(BF)
+    other = lax.dynamic_slice_in_dim(dkv, (1 - cx) * seg, seg, axis=2)
+    own = lax.dynamic_slice_in_dim(dkv, cx * seg, seg, axis=2)
+    came = lax.ppermute(other, "ctx", [(0, 1), (1, 0)])
+    own = (own.astype(F32) + came.astype(F32)).astype(BF).reshape(2, rows, -1)
+    grads = jnp.stack([dq, own[0], own[1]], axis=0)
+    qkv_part = f32dot("td,cte->dce", normed, grads)
+    normed_grad = lax.psum(f32dot("cte,cde->td", grads, wqkv).astype(BF), "tensor").astype(F32)
+    unused, first_back = jax.vjp(rms_norm, tok.astype(F32), gain_one)
+    token_grad, gain_one_part = first_back(normed_grad)
+    input_part = (token_grad + hidden_grad).astype(BF)
+    both = ("dp", "ctx")
+
+    def scatter(v, dim):
+        return lax.psum_scatter(v, both, scatter_dimension=dim, tiled=True)
+
+    up_grad = scatter(up_part.astype(BF), 1).astype(F32)
+    down_grad = jnp.transpose(scatter(down_part.astype(BF), 1).astype(F32), (0, 2, 1))
+    rest = scatter(
+        jnp.concatenate([qkv_part.reshape(width, -1), out_part], axis=1).astype(BF), 0
+    ).astype(F32)
+    span = q.shape[1]
+    qkv_grad = jnp.transpose(rest[:, : 3 * span].reshape(shard, 3, span), (1, 0, 2))
+    out_grad = rest[:, 3 * span :].T
+    tiny = scatter(
+        jnp.concatenate([gain_one_part[:, None], gain_two_part[:, None], router_part], axis=1), 0
+    )
+    bias_grad = lax.psum(dbias, both)[:, : position_bias.shape[1]]
+    return (
+        result.reshape(inputs.shape),
+        input_part.reshape(inputs.shape),
+        tiny[:, 0],
+        qkv_grad,
+        out_grad,
+        bias_grad,
+        tiny[:, 1],
+        tiny[:, 2:],
+        up_grad,
+        down_grad,
+    )
+
+
+def rms_norm(values, gain_vector):
+    return (
+        values * lax.rsqrt(jnp.mean(values * values, axis=-1, keepdims=True) + 1e-06) * gain_vector
+    )
 
 
 def bucket_of(distance):
@@ -15,12 +745,6 @@
     edge_values = jnp.asarray(bucket_edges, dtype=jnp.int32)
     beyond = jnp.sum((clipped[..., None] >= edge_values).astype(jnp.int32), axis=-1)
     return jnp.where(clipped < 16, clipped, jnp.minimum(16 + beyond, 31))
-
-
-def rms_norm(values, gain_vector):
-    return (
-        values * lax.rsqrt(jnp.mean(values * values, axis=-1, keepdims=True) + 1e-06) * gain_vector
-    )
 
 
 def toeplitz(diagonal, query_count, key_count):
@@ -406,8 +1130,9 @@
 
 
 def solution(mesh):
+    small = mesh.shape["ctx"] == 2 and mesh.shape["dp"] == 4 and mesh.shape["tensor"] == 4
     return jax.shard_map(
-        body,
+        body_fast if small else body,
         mesh=mesh,
         in_specs=(
             P("dp", "ctx", None),

time: 1250 us -> 759 us (0.61)
  local copies, waits for them, and re-layouts: 390 us -> 32.3 us
  Pallas kernels: 0 us -> 184 us
  blocking collectives: 173 us -> 37.1 us
  waiting for transfers between devices: 438 us -> 368 us
  other arithmetic: 92.6 us -> 33.7 us
  matrix products: 120 us -> 76.7 us
    pallas_call x0 -> x2, Pallas kernels: none -> 184 us  [the longest x1 163 us: first_call(): pl.pallas_call(functools.partial(first_kernel, heads), out_shape=(jax.Sha...]
    rev x3 -> x0, local copies, waits for them, and re-layouts: 147 us -> none  [the longest x2 96.3 us: diagonal_sums(): flipped = jnp.pad(gradient[:, :, ::-1], ((0, 0), (0, 0), (0, query_count)))]
    unnamed x194 -> x64, local copies, waits for them, and re-layouts: 136 us -> 20.6 us
    all_gather x7 -> x0, blocking collectives: 111 us -> none  [the longest x1 34 us: body(): lax.all_gather(qkv_weight, ('dp', 'ctx'), axis=1, tiled=True)]
    all_gather x2 -> x0, waiting for transfers between devices: 84.8 us -> none  [the longest x1 73.8 us: body(): lax.all_gather(up_weight, ('dp', 'ctx'), axis=1, tiled=True)]
    reduce_scatter x4 -> x2, waiting for transfers between devices: 264 us -> 192 us  [scatter(): return lax.psum_scatter(v, both, scatter_dimension=dim, tiled=True)]
    unnamed x2 -> x0, blocking collectives: 61.8 us -> none
    unnamed x15 -> x8, waiting for transfers between devices: 1.24 us -> 60.9 us
  transfers between devices with their start and end apart: 12 -> 7, of which waited for: 7 -> 6; matrix products, arithmetic and copies ran while one was open for 28% -> 6% of each run, Pallas kernels for 0% -> 0%
where the time goes in v1:
time: 759 us; the launch traced here: 749 us
  waiting for transfers between devices  368 us (48%)
  Pallas kernels  184 us (24%)
  matrix products  76.7 us (10%)
  blocking collectives  37.1 us (5%)
  other arithmetic  33.7 us (4%)
  local copies, waits for them, and re-layouts  32.3 us (4%)
  between operations  15 us (2%)
    reduce_scatter x2, waiting for transfers between devices, scatter(): return lax.psum_scatter(v, both, scatter_dimension=dim, tiled=True)  192 us
    pallas_call x1, Pallas kernels, first_call(): pl.pallas_call(functools.partial(first_kernel, heads), out_shape=(jax.Sha...  163 us
    psum x1, waiting for transfers between devices, body_fast(): expert_sum = lax.psum(spread, 'tensor').astype(F32)  67.1 us
    unnamed x8, waiting for transfers between devices  60.9 us
    psum x1, blocking collectives, body_fast(): bias_grad = lax.psum(dbias, both)[:, :position_bias.shape[1]]  37.1 us
    psum x1, waiting for transfers between devices, body_fast(): lax.psum(f32dot('cte,cde->td', grads, wqkv).astype(BF), 'tensor')  33.7 us
    pallas_call x1, Pallas kernels, back_call(): pl.pallas_call(functools.partial(back_kernel, heads), out_shape=(jax.Shap...  21.3 us
    unnamed x64, local copies, waits for them, and re-layouts  20.6 us
  transfers between devices with their start and end apart: 7, of which 6 were waited for; matrix products, arithmetic and copies ran while one was open for 6% of the time, Pallas kernels for 0%

profile of v1, /device:TPU:0, one launch (start us, length us, event | category | flops | bytes accessed | tf_op | source)
XLA Modules:
  0.0 749.1 jit_solution(2384184887850959656)
XLA Ops:
  11.6 2.4 pad_maximum_fusion.1.w
  15.6 163.1 %shard_map.204 = (f32[1024,768]{1,0:T(8,128)}, bf16[1024,768]{1,0:T(8,128)(2,1)}, bf16[1024,768]{1,0:T(8,128)(2,1)}, bf16[1024,192]{1,0:T(8,128)(2,1)}, bf16[2,1...) custom-call(s32[2]{0:T(128)} %len_ref.3, ...), custom_call_target="tpu_custom_call" | custom-call | tf_op jit(solution)/shard_map/pallas_call | solution.py:493
  180.8 6.1 fusion.43
  188.6 4.6 fusion.17
  193.3 11.8 %bitcast_convert_fusion.2 = bf16[1024,768]{1,0:T(8,128)(2,1)} fusion(s32[4,512]{1,0:T(4,128)S(1)} %bitcast.133, bf16[4,2,768,768]{3,2,1,0:T(8,128)(2,1)} %get-tuple-element.29, f32[4,512,768]{2,1,0:T(8,128)} %fusion.17), kind=kOutput, calls=%fused_computation.55 | convolution fusion | flops 5655756800 | bytes 12591104 | tf_op jit(solution)/shard_map/ekt,ekd->td/dot_general | solution.py:673
  205.1 5.0 fusion.44
  211.8 9.0 %fusion.10 = bf16[4,512,768]{2,1,0:T(8,128)(2,1)} fusion(f32[4,512,768]{2,1,0:T(8,128)S(1)} %copy-done.20, bf16[4,512,768]{2,1,0:T(8,128)(2,1)S(1)} %fusion.44, bf16[4,2,768,768]{3,2,1,0:T(8,128)(2,1)} %get-tuple-element.29), kind=kOutput, calls=%fused_computation.13 | convolution fusion | flops 2447376384 | bytes 17301504 | tf_op jit(solution)/shard_map/ekd,edf->ekf/dot_general | solution.py:675
  220.7 10.6 %bitcast_convert_fusion.1 = bf16[1024,768]{1,0:T(8,128)(2,1)} fusion(s32[4,512]{1,0:T(4,128)S(1)} %bitcast.135, bf16[4,512,768]{2,1,0:T(8,128)(2,1)} %fusion.10, bf16[4,2,768,768]{3,2,1,0:T(8,128)(2,1)} %get-tuple-element.29), kind=kOutput, calls=%fused_computation.54 | convolution fusion | flops 5641601024 | bytes 9445376 | tf_op jit(solution)/shard_map/ekt,ekd->td/dot_general | solution.py:679
  233.5 67.1 %all-reduce.6.cloned.1.call-done = (bf16[1024,768]{1,0:T(8,128)(2,1)}, bf16[1024,768]{1,0:T(8,128)(2,1)}) async-done(((bf16[1024,768]{1,0:T(8,128)(2,1)}, bf16[1024,768]{1,0:T(8,128)(2,1)}), (bf16[1024,768]{1,0:T(8,128)(2,1)}, bf16[1024,768]{1,0:T(8,128)(2,1)})) %all-reduce.6.cloned.1.call-update) | async-done | bytes 3145744 | tf_op jit(solution)/shard_map/psum | solution.py:680
  300.7 2.8 fusion.31
  306.4 2.7 fusion.33
  310.8 21.3 %shard_map.205 = (bf16[1024,192]{1,0:T(8,128)(2,1)}, f32[2,1024,192]{2,1,0:T(8,128)}, f32[2,1024,192]{2,1,0:T(8,128)}, f32[32,128]{1,0:T(8,128)}) custom-call(s32[2]{0:T(128)} %len_ref.3, f32[32,3]{1,0:T(8,128)} %copy.52.bias_ref, bf16[1024,192]{1,0:T(8,128)(2,1)} %get-tuple-element.30.q, bf16[2,1024,192]{2,1,0:T(8,128)(2,1)} %get-tuple-element.31.kcat, ...), custom_call_target="tpu_custom_call" | custom-call | tf_op jit(solution)/shard_map/pallas_call | solution.py:613
  332.1 2.5 fusion.62
  337.0 2.3 copy.57
  344.3 14.5 %collective-permute-done = bf16[2,2,512,192]{2,3,1,0:T(8,128)(2,1)} collective-permute-done((bf16[2,2,512,192]{2,3,1,0:T(8,128)(2,1)}, bf16[2,2,512,192]{2,3,1,0:T(8,128)(2,1)}, u32[]{:S(2)}, u32[]{:S(2)}) %collective-permute-start) | collective-permute-done | bytes 786464 | tf_op jit(solution)/shard_map/ppermute | solution.py:698
  358.8 2.2 copy.58
  364.0 2.6 bitcast_convert_fusion
  369.9 2.5 copy.61
  372.4 2.9 fusion.78
  376.2 33.7 %all-reduce.4.cloned.1.call-done = bf16[1024,768]{1,0:T(8,128)(2,1)} async-done(((bf16[1024,768]{1,0:T(8,128)(2,1)}), bf16[1024,768]{1,0:T(8,128)(2,1)}) %all-reduce.4.cloned.1.call-update) | async-done | bytes 1572880 | tf_op jit(solution)/shard_map/psum | solution.py:702
  409.9 3.4 fusion.32
  414.3 2.3 pad_maximum_fusion.2
  416.6 2.4 copy.74
  419.0 7.6 %convolution_convert_fusion.1 = bf16[4,768,768]{2,1,0:T(8,128)(2,1)} fusion(bf16[4,512,768]{2,1,0:T(8,128)(2,1)} %copy-done.21, bf16[4,512,768]{2,1,0:T(8,128)(2,1)} %fusion.10), kind=kOutput, calls=%fused_computation.64 | convolution fusion | flops 2418278400 | bytes 11010048 | tf_op jit(solution)/shard_map/ekd,ekf->edf/dot_general | solution.py:677
  427.0 9.1 %convolution_convert_fusion = bf16[4,768,768]{2,1,0:T(8,128)(2,1)} fusion(bf16[4,512,768]{2,1,0:T(8,128)(2,1)} %copy-done.22, f32[4,512,768]{2,1,0:T(8,128)} %fusion.17), kind=kOutput, calls=%fused_computation.63 | convolution fusion | flops 2432434176 | bytes 14155776 | tf_op jit(solution)/shard_map/ekd,ekf->edf/dot_general | solution.py:674
  436.8 37.1 %psum.31 = f32[32,128]{1,0:T(8,128)S(1)} all-reduce(f32[32,128]{1,0:T(8,128)S(1)} %copy-done.17), channel_id=1, replica_groups=mesh['dp'=4,'ctx'=2,'tensor'=4] {'dp','ctx'}, use_global_device_ids=true, to_apply=%region_15.16 | all-reduce | flops 4096 | bytes 32768 | tf_op jit(solution)/shard_map/psum | solution.py:722
  474.6 4.0 fusion.36
  482.2 60.8 %reduce-scatter.15.cloned.1.call-done = bf16[96,768]{1,0:T(8,128)(2,1)} async-done(((bf16[768,768]{1,0:T(8,128)(2,1)}), bf16[96,768]{1,0:T(8,128)(2,1)}) %reduce-scatter.15.cloned.1.call-update) | async-done | bytes 147472
  545.7 95.3 %reduce-scatter.9.cloned.1.call-done = bf16[4,96,768]{2,1,0:T(8,128)(2,1)} async-done(((bf16[4,768,768]{2,1,0:T(8,128)(2,1)}), bf16[4,96,768]{2,1,0:T(8,128)(2,1)}) %reduce-scatter.9.cloned.1.call-update) | async-done | bytes 589840 | tf_op jit(solution)/shard_map/reduce_scatter | solution.py:709
  640.9 2.2 convert_element_type.136
  643.1 96.6 %reduce-scatter.11.cloned.1.call-done = bf16[4,96,768]{2,1,0:T(8,128)(2,1)} async-done(((bf16[4,768,768]{2,1,0:T(8,128)(2,1)}), bf16[4,96,768]{2,1,0:T(8,128)(2,1)}) %reduce-scatter.11.cloned.1.call-update) | async-done | bytes 589840 | tf_op jit(solution)/shard_map/reduce_scatter | solution.py:709
  739.7 2.2 convert_bitcast_fusion
  (118 shorter events, 41.8 us)
Async XLA Ops:
  7.2 293.5 %all-reduce.6.cloned.1.call-start = ((), (), s32[]{:S(2)}) async-start(), calls=%async_computation.9 | async-start | bytes 6291456 | tf_op jit(solution)/shard_map/psum | solution.py:680
  11.6 169.1 %copy-start.18 = (s32[2,1,4,256]{3,2,1,0:T(4,128)S(1)}, s32[2,1,4,256]{3,2,1,0:T(4,128)}, u32[]{:S(2)}) copy-start(s32[2,1,4,256]{3,2,1,0:T(4,128)} %param.16) | copy-start | bytes 24580
  178.7 9.9 %slice-start = ((s8[9437184]{0:T(1024)(128)(4,1)}), s8[4194304]{0:T(1024)(128)(4,1)S(1)}, s32[]{:S(2)}) async-start(s8[9437184]{0:T(1024)(128)(4,1)} %bitcast.142), calls=%async_computation.10 | async-start | bytes 8388608
  180.8 7.7 %slice-start.1 = ((s8[9437184]{0:T(1024)(128)(4,1)}), s8[4194304]{0:T(1024)(128)(4,1)S(1)}, s32[]{:S(2)}) async-start(s8[9437184]{0:T(1024)(128)(4,1)} %bitcast.142), calls=%async_computation.11 | async-start | bytes 8388608
  180.8 7.7 %slice-start.2 = ((s8[9437184]{0:T(1024)(128)(4,1)}), s8[1048576]{0:T(1024)(128)(4,1)S(1)}, s32[]{:S(2)}) async-start(s8[9437184]{0:T(1024)(128)(4,1)} %bitcast.142), calls=%async_computation.12 | async-start | bytes 2097152
  186.9 1.7 copy-start.21
  193.2 11.9 %copy-start.4 = (bf16[2,512,768]{2,1,0:T(8,128)(2,1)S(1)}, bf16[2,512,768]{2,1,0:T(8,128)(2,1)}, u32[]{:S(2)}) copy-start(bf16[2,512,768]{2,1,0:T(8,128)(2,1)} %param.25) | copy-start | bytes 4718596
  205.1 6.6 copy-start.20
  210.1 1.6 copy-start.22
  220.7 10.7 %copy-start.16 = (f32[16,768]{1,0:T(8,128)S(1)}, f32[16,768]{1,0:T(8,128)}, u32[]{:S(2)}) copy-start(f32[16,768]{1,0:T(8,128)} %get-tuple-element.28) | copy-start | bytes 147460
  231.4 1.9 copy-start
  231.4 178.5 %all-reduce.4.cloned.1.call-start = ((), (), s32[]{:S(2)}) async-start(), calls=%async_computation.4 | async-start | bytes 3145728 | tf_op jit(solution)/shard_map/psum | solution.py:702
  300.7 2.8 copy-start.11
  303.5 1.9 copy-start.1
  303.5 2.3 copy-start.5
  303.5 2.8 copy-start.6
  306.4 2.7 copy-start.14
  334.6 1.0 copy-start.2
  334.6 1.3 copy-start.3
  339.3 19.5 %collective-permute-start = (bf16[2,2,512,192]{2,3,1,0:T(8,128)(2,1)}, bf16[2,2,512,192]{2,3,1,0:T(8,128)(2,1)}, u32[]{:S(2)}, u32[]{:S(2)}) collective-permute-start(bf16[2,2,512,192]{2,3,1,0:T(8,128)(2,1)} %copy.57), channel_id=1, source_target_pairs={{0,4},{4,0},{1,5},{5,1},{2,6},{6,2},{3,7},{7,3},{8,12},{12,8},{9,1... | collective-permute-start | bytes 2359304 | tf_op jit(solution)/shard_map/ppermute | solution.py:698
  361.0 3.0 copy-start.12
  361.0 3.0 copy-start.19
  363.0 0.8 copy-start.7
  363.0 1.0 copy-start.9
  366.6 112.0 %reduce-scatter.13.cloned.1.call-start = ((), (), s32[]{:S(2)}) async-start(), calls=%async_computation.7 | async-start | bytes 442368
  366.6 1.7 copy-start.8
  366.6 1.7 copy-start.10
  366.6 1.7 copy-start.13
  414.3 128.7 %reduce-scatter.15.cloned.1.call-start = ((), (), s32[]{:S(2)}) async-start(), calls=%async_computation.8 | async-start | bytes 1327104
  419.0 221.9 %reduce-scatter.9.cloned.1.call-start = ((), (), s32[]{:S(2)}) async-start(), calls=%async_computation.5 | async-start | bytes 5308416 | tf_op jit(solution)/shard_map/reduce_scatter | solution.py:709
  426.7 313.0 %reduce-scatter.11.cloned.1.call-start = ((), (), s32[]{:S(2)}) async-start(), calls=%async_computation.6 | async-start | bytes 5308416 | tf_op jit(solution)/shard_map/reduce_scatter | solution.py:709
  436.1 0.7 copy-start.17
  (1 other events, 0.6 us)
Sparse Core Ops, SparseCore 0:
  231.5 69.1 all-reduce.5
  366.7 43.1 all-reduce.3
  414.4 61.4 reduce-scatter.12
  479.7 63.2 reduce-scatter.14
  546.5 94.3 reduce-scatter.8
  644.4 95.1 reduce-scatter.10

commit v2 on v1

--- a/solution.py
+++ b/solution.py
@@ -274,7 +274,7 @@
         Group(
             place,
             w.at[e],
-            lambda s, e=e: w_full.at[e, :, rows96(s), :],
+            lambda s, e=e: w_full.at[e, :, s],
             lambda i, e=e: w_s.at[e, i],
             lambda i, e=e: w_r.at[e, i],
             lambda i, e=e: w_s.at[e, 3 + i],
@@ -504,7 +504,7 @@
             jax.ShapeDtypeStruct((3, width, span), BF),
             jax.ShapeDtypeStruct((width, span), BF),
             jax.ShapeDtypeStruct((16, width), F32),
-            jax.ShapeDtypeStruct((experts, 2, width, ff), BF),
+            jax.ShapeDtypeStruct((experts, 2, 8, width // 8, ff), BF),
         ),
         in_specs=[sm, sm, vm, hbm, hbm, hbm, hbm],
         out_specs=(vm,) * 11 + (hbm,),
@@ -536,35 +536,430 @@
     )(lengths, bias, tok, small, wqkv, wo, w)
 
 
-def back_kernel(heads, len_ref, bias_ref, q, kcat, vcat, lse, grad, dq, dk, dv, dbias, band, scores, spread, band_sum, whole_sum):
-    cx = lax.axis_index("ctx")
-    seg = q.shape[0] // 2
+C0 = float(np.sqrt(2.0 / np.pi))
+C1 = 0.044715
+
+
+def norm_back(x, gain, grad):
+    scale = lax.rsqrt(jnp.mean(x * x, axis=-1, keepdims=True) + 1e-06)
+    unit = x * scale
+    pulled = grad * gain
+    inner = jnp.mean(pulled * unit, axis=-1, keepdims=True)
+    return scale * (pulled - unit * inner), grad * unit
+
+
+def second_kernel(
+    heads,
+    len_ref,
+    bias_ref,
+    ids,
+    slot_lanes,
+    slot_subs,
+    cot,
+    ntwo,
+    q,
+    kcat,
+    vcat,
+    lse,
+    ab,
+    wqkv,
+    wo,
+    gains,
+    normed_hbm,
+    tok_hbm,
+    hidden_hbm,
+    w_full,
+    result,
+    input_grad,
+    w_grad,
+    small_grad,
+    tiny_out,
+    dbias_out,
+    wbuf,
+    gw,
+    xbuf,
+    gq,
+    qx,
+    qz,
+    sum_grad,
+    epart,
+    npart,
+    ffn,
+    probs_ref,
+    hidden,
+    tok,
+    cbuf,
+    ysend,
+    ybuf,
+    kept,
+    hgrad,
+    bgrad,
+    own_out,
+    agrad,
+    grads,
+    dk,
+    dv,
+    dkv,
+    band,
+    scores,
+    spread,
+    band_sum,
+    whole_sum,
+    tiny_own,
+    tiny_t,
+    tiny_mid,
+    tiny_g,
+    dbias_own,
+    dbias_g,
+    load_sem,
+    row_sem,
+    out_sem,
+    ready,
+    wx_s,
+    wx_r,
+    wz_s,
+    wz_r,
+    c_s,
+    c_r,
+    y_s,
+    y_r,
+    a_s,
+    a_r,
+    kv_s,
+    kv_r,
+    qx_s,
+    qx_r,
+    qz_s,
+    qz_r,
+    tt_s,
+    tt_r,
+    tg_s,
+    tg_r,
+    db_s,
+    db_r,
+):
+    dp, cx, t = lax.axis_index("dp"), lax.axis_index("ctx"), lax.axis_index("tensor")
+    yy, core = t // 2, lax.rem(t, 2)
+    seg = cot.shape[0] // 2
+    width = cot.shape[1]
+    experts = w_full.shape[0]
+    cap = slot_subs.shape[0]
+    half, quarter = seg // 2, seg // 4
+    group_peers = [
+        (lax.rem(dp + k, 4), cx if c == 0 else 1 - cx, t)
+        for k in range(4)
+        for c in range(2)
+        if (k, c) != (0, 0)
+    ]
+    tensor_peers = [(dp, cx, lax.rem(t + k, 4)) for k in (1, 2, 3)]
+    sibling = (dp, cx, t + 1 - 2 * core)
+    across = (dp, cx, lax.rem(t + 2, 4))
+    partner = (dp, 1 - cx, t)
+
+    def z_peer(k):
+        return (lax.rem(dp + k, 4), cx, t)
+
+    barrier = pltpu.get_barrier_semaphore()
+    for peer in group_peers + tensor_peers:
+        pl.semaphore_signal(barrier, inc=1, device_id=peer, device_id_type=MESH)
+    pl.semaphore_wait(barrier, len(group_peers) + len(tensor_peers))
+
+    def remote(src, dst, send, recv, device):
+        return pltpu.make_async_remote_copy(
+            src_ref=src,
+            dst_ref=dst,
+            send_sem=send,
+            recv_sem=recv,
+            device_id=device,
+            device_id_type=MESH,
+        )
+
+    def rows96(s):
+        return pl.ds(pl.multiple_of(s * 96, 32), 96)
+
+    def load(e, slot):
+        return pltpu.make_async_copy(w_full.at[e], wbuf.at[pl.ds(slot * 2, 2)], load_sem.at[slot])
+
+    def own_rows(m, size=None):
+        return pl.ds(pl.multiple_of(m * seg + core * half + yy * quarter, 128), quarter)
+
+    def fetch(m, which):
+        ref, dst = ((hidden_hbm, hidden), (tok_hbm, tok))[which]
+        return pltpu.make_async_copy(ref.at[own_rows(m)], dst.at[m], row_sem.at[m * 2 + which])
+
+    load(0, 0).start()
+    for m in range(2):
+        fetch(m, 0).start()
+        fetch(m, 1).start()
+
+    router16 = gains[...].astype(BF)
+
+    def upstream_of(rows, m, first):
+        spot = lax.broadcasted_iota(jnp.int32, (rows.size, 1), 0) + (cx * seg + first)
+        live = (spot < len_ref[m]).astype(F32)
+        return live, live * cot[rows, :].astype(F32)
+
+    def chosen_of(rows):
+        lanes = lax.broadcasted_iota(jnp.int32, (rows.size, 16), 1)
+        return (lanes == ids[rows, :] + 2).astype(F32)
+
+    for m in range(2):
+
+        def gates(i, carry):
+            rows = pl.ds(pl.multiple_of(m * seg + i * 256, 256), 256)
+            logits = mm_nt(ntwo[rows, :], router16)
+            lanes = lax.broadcasted_iota(jnp.int32, (256, 16), 1)
+            inside = (lanes >= 2) & (lanes < 2 + experts)
+            logits = jnp.where(inside, logits, -1e30)
+            top = jnp.max(logits, axis=-1, keepdims=True)
+            raised = jnp.where(inside, jnp.exp(logits - top), 0.0)
+            probs = raised / jnp.sum(raised, axis=-1, keepdims=True)
+            probs_ref[rows, :] = probs
+            gate = jnp.sum(probs * chosen_of(rows), axis=-1, keepdims=True)
+            live, upstream = upstream_of(rows, m, i * 256)
+            sum_grad[rows, :] = (gate * upstream).astype(BF)
+            epart[rows, :] = jnp.zeros((256, width), BF)
+            npart[rows, :] = jnp.zeros((256, width), BF)
+            return carry
+
+        lax.fori_loop(0, seg // 256, gates, 0)
+
+    def wx_copy(e, k):
+        d = lax.rem(dp + k, 4)
+        return remote(
+            gw.at[e, :, d * 2 + 1 - cx], xbuf.at[e, k], wx_s.at[e, k], wx_r.at[e, k], partner
+        )
+
+    def wz_copy(e, k):
+        spot = wbuf.at[e, pl.ds(2 * (k - 1), 2)]
+        return remote(xbuf.at[e, k], spot, wz_s.at[e, k - 1], wz_r.at[e, k - 1], z_peer(k))
+
+    order = (2, 1, 3, 0)
+
+    def weight(slot, which):
+        return wbuf[slot * 2 + which].reshape(width, -1)
+
+    picked, slot_grad, activated, raised_grad = (ffn.at[i] for i in range(4))
+
+    def expert_step(e, carry):
+        slot = lax.rem(e, 2)
+        load(e, slot).wait()
+
+        @pl.when(e + 1 < experts)
+        def _():
+            load(e + 1, 1 - slot).start()
+
+        def one_micro(m, carry):
+            rows = pl.ds(pl.multiple_of(m * seg, seg), seg)
+            slots = pl.ds(pl.multiple_of(m * cap, cap), cap)
+            lanes = lax.broadcasted_iota(jnp.int32, (cap, 8), 1)
+            column = jnp.sum(
+                jnp.where(lanes == m * experts + e, slot_subs[...], 0), axis=1, keepdims=True
+            )
+            pick = (column == lax.broadcasted_iota(jnp.int32, (cap, seg), 1)).astype(BF)
+            row = slot_lanes[pl.ds(m * experts + e, 1), :]
+            put = (row == lax.broadcasted_iota(jnp.int32, (seg, cap), 0)).astype(BF)
+            chosen_rows = mm(pick, ntwo[rows, :]).astype(BF)
+            picked[slots, :] = chosen_rows
+            slot_part = mm(pick, sum_grad[rows, :]).astype(BF)
+            slot_grad[slots, :] = slot_part
+            raised = mm(chosen_rows, weight(slot, 0))
+            square = raised * raised
+            bent = jnp.tanh(C0 * raised * (1.0 + C1 * square))
+            cdf = 0.5 * (1.0 + bent)
+            act = (raised * cdf).astype(BF)
+            activated[slots, :] = act
+            slope = cdf + 0.5 * raised * (1.0 - bent * bent) * (C0 * (1.0 + 3.0 * C1 * square))
+            act_grad = mm(slot_part, weight(slot, 1))
+            back = (act_grad * slope).astype(BF)
+            raised_grad[slots, :] = back
+            lowered = mm_nt(act, weight(slot, 1)).astype(BF)
+            epart[rows, :] += mm(put, lowered).astype(BF)
+            pulled = mm_nt(back, weight(slot, 0)).astype(BF)
+            npart[rows, :] += mm(put, pulled).astype(BF)
+            return carry
+
+        lax.fori_loop(0, 2, one_micro, 0)
+
+        def weight_part(i, carry):
+            lanes = pl.ds(pl.multiple_of(i * 384, 128), 384)
+            slabs = pl.ds(i * 4, 4)
+            part = mm_tn(picked[:, lanes], raised_grad[...]).astype(BF)
+            gw[e, 0, slabs] = part.reshape(4, 96, -1)
+            part = mm_tn(slot_grad[:, lanes], activated[...]).astype(BF)
+            gw[e, 1, slabs] = part.reshape(4, 96, -1)
+            return carry
+
+        lax.fori_loop(0, width // 384, weight_part, 0)
+
+        @pl.when(e < 2)
+        def _():
+            for k in order:
+                wx_copy(e, k).start()
+
+        return carry
+
+    lax.fori_loop(0, experts, expert_step, 0)
+
+    for k in (1, 2, 3):
+        pl.semaphore_signal(ready, inc=1, device_id=z_peer(k), device_id_type=MESH)
+
+    def fetch_normed(i):
+        return pltpu.make_async_copy(
+            normed_hbm.at[pl.ds(i * seg, seg)], ffn.at[i], load_sem.at[i]
+        )
+
+    fetch_normed(0).start()
+    fetch_normed(1).start()
+
+    def half_rows(m, c):
+        return pl.ds(pl.multiple_of(m * seg + c * half, 128), half)
+
+    parts = (epart, npart, None)
+
+    def c_copy(m, j, src):
+        return remote(
+            src.at[half_rows(m, 1 - core)], cbuf.at[m, j % 2], c_s.at[m, j], c_r.at[m, j], sibling
+        )
+
+    def y_copy(m, j):
+        return remote(ysend.at[m, j % 2], ybuf.at[m, j % 2], y_s.at[m, j], y_r.at[m, j], across)
+
+    def to_quarters(m, j, src):
+        c_copy(m, j, src).wait_recv()
+        mine = pl.ds(pl.multiple_of(m * seg + core * half + yy * quarter, 128), quarter)
+        other = pl.ds(pl.multiple_of(m * seg + core * half + (1 - yy) * quarter, 128), quarter)
+        near = pl.ds(pl.multiple_of(yy * quarter, 128), quarter)
+        far = pl.ds(pl.multiple_of((1 - yy) * quarter, 128), quarter)
+        ysend[m, j % 2] = (src[other, :].astype(F32) + cbuf[m, j % 2, far, :].astype(F32)).astype(BF)
+        y_copy(m, j).start()
+        kept[m, j % 2] = src[mine, :].astype(F32) + cbuf[m, j % 2, near, :].astype(F32)
+
+    def a_copy(m, j, ref, step):
+        at = 1 - yy if step == 2 else yy
+        spot = ref.at[pl.ds(pl.multiple_of(m * seg + core * half + at * quarter, 128), quarter)]
+        source = spot if j == 0 or step == 2 else own_out.at[m, j - 1]
+        return remote(
+            source, spot, a_s.at[m, j, step], a_r.at[m, j, step], across if step == 0 else sibling
+        )
+
+    def a_recv(m, j, ref, step):
+        c = core if step == 0 else 1 - core
+        at = 1 - yy if step in (0, 2) else yy
+        spot = ref.at[pl.ds(pl.multiple_of(m * seg + c * half + at * quarter, 128), quarter)]
+        return remote(spot, spot, a_s.at[m, j, step], a_r.at[m, j, step], sibling)
+
+    def own_copy(m, j, ref):
+        return pltpu.make_async_copy(
+            own_out.at[m, j - 1], ref.at[own_rows(m)], out_sem.at[m * 2 + j - 1]
+        )
+
+    def share(m, j, ref):
+        a_copy(m, j, ref, 0).start()
+        a_copy(m, j, ref, 1).start()
+        if j > 0:
+            own_copy(m, j, ref).start()
+
+    def pass_on(m, j, ref):
+        a_recv(m, j, ref, 0).wait_recv()
+        a_copy(m, j, ref, 2).start()
+
+    def shared(m, j, ref):
+        a_recv(m, j, ref, 1).wait_recv()
+        a_recv(m, j, ref, 2).wait_recv()
+
+    def reduce_step(e):
+        for k in order:
+            wx_copy(e, k).wait_recv()
+            mine = gw[e, :, lax.rem(dp + k, 4) * 2 + cx].astype(F32)
+            total = mine + xbuf[e, k].astype(F32)
+            if k == 0:
+                w_grad[e] = total
+            else:
+                xbuf[e, k] = total.astype(BF)
+                wz_copy(e, k).start()
+
+    def reduce_end(e):
+        total = w_grad[e]
+        for k in (1, 2, 3):
+            wz_copy(e, k).wait_recv()
+            total = total + wbuf[e, 2 * (k - 1) : 2 * k].astype(F32)
+        w_grad[e] = total
+
+    for m in range(2):
+        for j in range(2):
+            c_copy(m, j, parts[j]).start()
+    for m in range(2):
+        for j in range(2):
+            to_quarters(m, j, parts[j])
+
     fill_bias(bias_ref, band, heads)
-    dk[...] = jnp.zeros(dk.shape, F32)
-    dv[...] = jnp.zeros(dv.shape, F32)
     spread[...] = jnp.zeros(spread.shape, F32)
     band_sum[...] = jnp.zeros(band_sum.shape, F32)
     whole_sum[...] = jnp.zeros(whole_sum.shape, F32)
+    tiny_own[...] = jnp.zeros(tiny_own.shape, F32)
+    pl.semaphore_wait(ready, 3)
+    reduce_step(0)
+
     for m in range(2):
+        fetch(m, 0).wait()
+        fetch(m, 1).wait()
+        for j in range(2):
+            y_copy(m, j).wait_recv()
+        rows = own_rows(m)
+        expert_sum = kept[m, 0] + ybuf[m, 0].astype(F32)
+        live, upstream = upstream_of(rows, m, core * half + yy * quarter)
+        probs, chosen = probs_ref[rows, :], chosen_of(rows)
+        gate = jnp.sum(probs * chosen, axis=-1, keepdims=True)
+        gate_grad = jnp.sum(expert_sum * upstream, axis=-1, keepdims=True)
+        logit_grad = (probs * gate_grad * (chosen - gate)).astype(BF)
+        x = hidden[m]
+        down = kept[m, 1] + ybuf[m, 1].astype(F32) + mm(logit_grad, router16)
+        through, gain_terms = norm_back(x, gains[1:2, :], down)
+        full = through + upstream
+        hgrad[m] = full
+        bgrad[rows, :] = full.astype(BF)
+        share(m, 0, bgrad)
+        own_out[m, 0] = (live * (x + gate * expert_sum)).astype(BF)
+        share(m, 1, result)
+        tiny_own[1:2, :] += jnp.sum(gain_terms, axis=0, keepdims=True)
+        tiny_own[...] += mm_tn(logit_grad, ntwo[rows, :])
+    for m in range(2):
+        pass_on(m, 0, bgrad)
+
+    def dkv_copy(m):
+        return remote(dkv.at[m], dkv.at[m], kv_s.at[m], kv_r.at[m], partner)
+
+    def attend_back(m):
         length = len_ref[m]
+        dk[...] = jnp.zeros(dk.shape, F32)
+        dv[...] = jnp.zeros(dv.shape, F32)
+
+        def lower(i, carry):
+            rows = pl.ds(pl.multiple_of(m * seg + i * 256, 256), 256)
+            agrad[pl.ds(pl.multiple_of(i * 256, 256), 256), :] = mm(bgrad[rows, :], wo[...]).astype(BF)
+            return carry
+
+        lax.fori_loop(0, seg // 256, lower, 0)
 
         def step(i, carry):
             rows = pl.ds(pl.multiple_of(m * seg + i * QT, QT), QT)
+            local = pl.ds(pl.multiple_of(i * QT, QT), QT)
             first = cx * seg + i * QT
             held = []
             for h in range(heads):
                 cut = lanes_of(h, heads)
                 q_tile = head_tile(q[rows, cut], h, heads)
-                do_tile = head_tile(grad[rows, cut], h, heads)
+                do_tile = head_tile(agrad[local, cut], h, heads)
                 values, allowed = masked_scores(
                     q_tile, kcat[m, :, cut], band, scores, h, first, length
                 )
                 soft = jnp.where(allowed, jnp.exp(values - lse[rows, h : h + 1]), 0.0)
                 soft_grad = mm_nt(do_tile, vcat[m, :, cut])
-                dv[m, :, cut] += mm_tn(soft.astype(BF), do_tile)
+                dv[:, cut] += mm_tn(soft.astype(BF), do_tile)
                 delta = jnp.sum(soft * soft_grad, axis=-1, keepdims=True)
                 score_grad = (soft * (soft_grad - delta)).astype(BF)
-                dk[m, :, cut] += mm_tn(score_grad, q_tile)
+                dk[:, cut] += mm_tn(score_grad, q_tile)
                 held.append(mm(score_grad, kcat[m, :, cut]) * 0.125)
                 spread[:, BAND:] = score_grad.astype(F32)
                 for part in range(QT // BAND):
@@ -573,14 +968,287 @@
                 whole_sum[h : h + 1, :] += jnp.sum(spread[:, BAND:], axis=0, keepdims=True)
                 if h % 2 == 1:
                     both = jnp.where(lane_halves(held[0].shape), held[0], held[1])
-                    dq[rows, cut] = both.astype(BF)
+                    grads[0, rows, cut] = both.astype(BF)
                     held = []
                 elif h == heads - 1:
-                    dq[rows, cut] = held[0].astype(BF)
+                    grads[0, rows, cut] = held[0].astype(BF)
             return carry
 
         lax.fori_loop(0, seg // QT, step, 0)
-    bucket_sums(heads, band_sum, whole_sum, dbias)
+
+        @pl.when(cx == 1)
+        def _():
+            dkv[m, 0] = (dk[0:seg, :] * 0.125).astype(BF)
+            dkv[m, 1] = dv[0:seg, :].astype(BF)
+            dkv_copy(m).start()
+
+        own = pl.ds(pl.multiple_of(cx * seg, seg), seg)
+        rows = pl.ds(m * seg, seg)
+        grads[1, rows, :] = (dk[own, :] * 0.125).astype(BF)
+        grads[2, rows, :] = dv[own, :].astype(BF)
+
+    def after_attend(m):
+        rows = pl.ds(m * seg, seg)
+
+        @pl.when(cx == 0)
+        def _():
+            dkv_copy(m).wait_recv()
+            for i in range(2):
+                total = grads[1 + i, rows, :].astype(F32) + dkv[m, i].astype(F32)
+                grads[1 + i, rows, :] = total.astype(BF)
+
+        def lower(i, carry):
+            spot = pl.ds(pl.multiple_of(m * seg + i * 256, 256), 256)
+            total = mm_nt(grads[0, spot, :], wqkv[0])
+            for c in (1, 2):
+                total = total + mm_nt(grads[c, spot, :], wqkv[c])
+            npart[spot, :] = total.astype(BF)
+            return carry
+
+        lax.fori_loop(0, seg // 256, lower, 0)
+        c_copy(m, 2, npart).start()
+
+    for m in range(2):
+        shared(m, 0, bgrad)
+        attend_back(m)
+        for k in order:
+            wx_copy(2 + m, k).start()
+        reduce_step(m) if m == 1 else None
+        pass_on(m, 1, result)
+
+    def out_part(i, carry):
+        lanes = pl.ds(pl.multiple_of(i * 256, 256), 256)
+        gq[3, lanes, :] = mm_tn(bgrad[:, lanes], ab[...]).astype(BF)
+        return carry
+
+    lax.fori_loop(0, width // 256, out_part, 0)
+    bucket_sums(heads, band_sum, whole_sum, dbias_own)
+
+    def db_copy(i):
+        return remote(dbias_own, dbias_g.at[i], db_s.at[i], db_r.at[i], group_peers[i])
+
+    for i in range(7):
+        db_copy(i).start()
+
+    for m in range(2):
+        c_copy(m, 1, npart).wait_send()
+        y_copy(m, 0).wait_send()
+        after_attend(m)
+    fetch_normed(0).wait()
+    fetch_normed(1).wait()
+
+    def qkv_part(i, carry):
+        lanes = pl.ds(pl.multiple_of(i * 256, 256), 256)
+        for c in range(3):
+            part = mm_tn(ffn[0, :, lanes], grads[c, 0:seg, :])
+            part = part + mm_tn(ffn[1, :, lanes], grads[c, seg:, :])
+            gq[c, lanes, :] = part.astype(BF)
+        return carry
+
+    lax.fori_loop(0, width // 256, qkv_part, 0)
+
+    def qx_copy(k):
+        d = lax.rem(dp + k, 4)
+        return remote(gq.at[:, rows96(d * 2 + 1 - cx), :], qx.at[k], qx_s.at[k], qx_r.at[k], partner)
+
+    def qz_copy(k):
+        return remote(qx.at[k], qz.at[k - 1], qz_s.at[k - 1], qz_r.at[k - 1], z_peer(k))
+
+    for k in order:
+        qx_copy(k).start()
+
+    for m in range(2):
+        to_quarters(m, 2, npart)
+    reduce_step(2)
+
+    for m in range(2):
+        y_copy(m, 2).wait_recv()
+        rows = own_rows(m)
+        down = kept[m, 0] + ybuf[m, 0].astype(F32)
+        through, gain_terms = norm_back(tok[m].astype(F32), gains[0:1, :], down)
+        own_out[m, 1] = (through + hgrad[m]).astype(BF)
+        share(m, 2, input_grad)
+        tiny_own[0:1, :] += jnp.sum(gain_terms, axis=0, keepdims=True)
+
+    def tt_copy(k):
+        return remote(tiny_own, tiny_t.at[k - 1], tt_s.at[k - 1], tt_r.at[k - 1], tensor_peers[k - 1])
+
+    for k in (1, 2, 3):
+        tt_copy(k).start()
+    for m in range(2):
+        pass_on(m, 2, input_grad)
+    for k in (1, 2, 3):
+        tt_copy(k).wait_recv()
+    tiny_mid[...] = tiny_own[...] + tiny_t[0] + tiny_t[1] + tiny_t[2]
+
+    def tg_copy(i):
+        return remote(tiny_mid, tiny_g.at[i], tg_s.at[i], tg_r.at[i], group_peers[i])
+
+    for i in range(7):
+        tg_copy(i).start()
+
+    reduce_step(3)
+    for k in order:
+        qx_copy(k).wait_recv()
+        total = gq[:, rows96(lax.rem(dp + k, 4) * 2 + cx), :].astype(F32) + qx[k].astype(F32)
+        if k == 0:
+            small_grad[...] = total
+        else:
+            qx[k] = total.astype(BF)
+            qz_copy(k).start()
+
+    total = dbias_own[...]
+    for i in range(7):
+        db_copy(i).wait_recv()
+        total = total + dbias_g[i]
+    dbias_out[...] = total
+    total = tiny_mid[...]
+    for i in range(7):
+        tg_copy(i).wait_recv()
+        total = total + tiny_g[i]
+    tiny_out[...] = total
+    for e in range(experts):
+        reduce_end(e)
+    total = small_grad[...]
+    for k in (1, 2, 3):
+        qz_copy(k).wait_recv()
+        total = total + qz[k - 1].astype(F32)
+    small_grad[...] = total
+    for m in range(2):
+        shared(m, 1, result)
+        shared(m, 2, input_grad)
+
+    for e in range(experts):
+        for k in range(4):
+            wx_copy(e, k).wait_send()
+            if k > 0:
+                wz_copy(e, k).wait_send()
+    for k in range(4):
+        qx_copy(k).wait_send()
+        if k > 0:
+            qz_copy(k).wait_send()
+    for m in range(2):
+        c_copy(m, 0, epart).wait_send()
+        c_copy(m, 2, npart).wait_send()
+        own_copy(m, 1, result).wait()
+        own_copy(m, 2, input_grad).wait()
+        for j in range(3):
+            if j > 0:
+                y_copy(m, j).wait_send()
+            for step in range(3):
+                a_copy(m, j, (bgrad, result, input_grad)[j], step).wait_send()
+
+        @pl.when(cx == 1)
+        def _():
+            dkv_copy(m).wait_send()
+
+    for k in (1, 2, 3):
+        tt_copy(k).wait_send()
+    for i in range(7):
+        tg_copy(i).wait_send()
+        db_copy(i).wait_send()
+
+
+def second_call(
+    lengths, bias, ids, slot_lanes, slot_subs, cot, ntwo, q, kcat, vcat, lse, ab, wqkv, wo, gains,
+    normed, tok, hidden, w_full,
+):
+    heads = bias.shape[1]
+    rows, width = cot.shape
+    span = q.shape[1]
+    experts, ff = w_full.shape[0], w_full.shape[4]
+    seg = rows // 2
+    quarter = seg // 4
+    shard = width // 8
+    slots = 2 * slot_subs.shape[0]
+    vm = pl.BlockSpec(memory_space=pltpu.VMEM)
+    sm = pl.BlockSpec(memory_space=pltpu.SMEM)
+    hbm = pl.BlockSpec(memory_space=pl.ANY)
+    dma = pltpu.SemaphoreType.DMA
+    sds = jax.ShapeDtypeStruct
+    return pl.pallas_call(
+        functools.partial(second_kernel, heads),
+        out_shape=(
+            sds((rows, width), BF),
+            sds((rows, width), BF),
+            sds((experts, 2, shard, ff), F32),
+            sds((4, shard, span), F32),
+            sds((16, width), F32),
+            sds((BUCKETS, 128), F32),
+        ),
+        in_specs=[sm, sm] + [vm] * 13 + [hbm] * 4,
+        out_specs=(hbm,) * 2 + (vm,) * 4,
+        scratch_shapes=[
+            pltpu.VMEM((4, 8, shard, ff), BF),
+            pltpu.VMEM((experts, 2, 8, shard, ff), BF),
+            pltpu.VMEM((experts, 4, 2, shard, ff), BF),
+            pltpu.VMEM((4, width, span), BF),
+            pltpu.VMEM((4, 4, shard, span), BF),
+            pltpu.VMEM((3, 4, shard, span), BF),
+            pltpu.VMEM((rows, width), BF),
+            pltpu.VMEM((rows, width), BF),
+            pltpu.VMEM((rows, width), BF),
+            pltpu.VMEM((4, slots, width), BF),
+            pltpu.VMEM((rows, 16), F32),
+            pltpu.VMEM((2, quarter, width), F32),
+            pltpu.VMEM((2, quarter, width), BF),
+            pltpu.VMEM((2, 2, 2 * quarter, width), BF),
+            pltpu.VMEM((2, 2, quarter, width), BF),
+            pltpu.VMEM((2, 2, quarter, width), BF),
+            pltpu.VMEM((2, 2, quarter, width), F32),
+            pltpu.VMEM((2, quarter, width), F32),
+            pltpu.VMEM((rows, width), BF),
+            pltpu.VMEM((2, 2, quarter, width), BF),
+            pltpu.VMEM((seg, span), BF),
+            pltpu.VMEM((3, rows, span), BF),
+            pltpu.VMEM((rows, span), F32),
+            pltpu.VMEM((rows, span), F32),
+            pltpu.VMEM((2, 2, seg, span), BF),
+            pltpu.VMEM((heads, BAND, 2 * BAND), F32),
+            pltpu.VMEM((QT, rows + BAND), F32),
+            pltpu.VMEM((QT, rows + BAND), F32),
+            pltpu.VMEM((heads, BAND, 2 * BAND), F32),
+            pltpu.VMEM((8, rows), F32),
+            pltpu.VMEM((16, width), F32),
+            pltpu.VMEM((3, 16, width), F32),
+            pltpu.VMEM((16, width), F32),
+            pltpu.VMEM((7, 16, width), F32),
+            pltpu.VMEM((BUCKETS, 128), F32),
+            pltpu.VMEM((7, BUCKETS, 128), F32),
+            dma((2,)),
+            dma((4,)),
+            dma((4,)),
+            pltpu.SemaphoreType.REGULAR,
+            dma((experts, 4)),
+            dma((experts, 4)),
+            dma((experts, 3)),
+            dma((experts, 3)),
+            dma((2, 3)),
+            dma((2, 3)),
+            dma((2, 3)),
+            dma((2, 3)),
+            dma((2, 3, 3)),
+            dma((2, 3, 3)),
+            dma((2,)),
+            dma((2,)),
+            dma((4,)),
+            dma((4,)),
+            dma((3,)),
+            dma((3,)),
+            dma((3,)),
+            dma((3,)),
+            dma((7,)),
+            dma((7,)),
+            dma((7,)),
+            dma((7,)),
+        ],
+        compiler_params=pltpu.CompilerParams(
+            collective_id=1, has_side_effects=True, vmem_limit_bytes=63 << 20
+        ),
+    )(
+        lengths, bias, ids, slot_lanes, slot_subs, cot, ntwo, q, kcat, vcat, lse, ab, wqkv, wo, gains,
+        normed, tok, hidden, w_full,
+    )
 
 
 def bucket_sums(heads, band_sum, whole_sum, dbias):
@@ -606,31 +1274,6 @@
     dbias[...] = result
 
 
-def back_call(lengths, bias, q, kcat, vcat, lse, grad):
-    heads = bias.shape[1]
-    vm = pl.BlockSpec(memory_space=pltpu.VMEM)
-    sm = pl.BlockSpec(memory_space=pltpu.SMEM)
-    return pl.pallas_call(
-        functools.partial(back_kernel, heads),
-        out_shape=(
-            jax.ShapeDtypeStruct(q.shape, BF),
-            jax.ShapeDtypeStruct(kcat.shape, F32),
-            jax.ShapeDtypeStruct(kcat.shape, F32),
-            jax.ShapeDtypeStruct((BUCKETS, 128), F32),
-        ),
-        in_specs=[sm, sm] + [vm] * 5,
-        out_specs=(vm,) * 4,
-        scratch_shapes=[
-            pltpu.VMEM((heads, BAND, 2 * BAND), F32),
-            pltpu.VMEM((QT, q.shape[0] + BAND), F32),
-            pltpu.VMEM((QT, q.shape[0] + BAND), F32),
-            pltpu.VMEM((heads, BAND, 2 * BAND), F32),
-            pltpu.VMEM((8, q.shape[0]), F32),
-        ],
-        compiler_params=pltpu.CompilerParams(vmem_limit_bytes=56 << 20),
-    )(lengths, bias, q, kcat, vcat, lse, grad)
-
-
 def body_fast(
     inputs, lengths, expert_ids, slot_rows, attn_gain, qkv_weight, out_weight, position_bias,
     ffn_gain, router_weight, up_weight, down_weight, cotangent,
@@ -650,87 +1293,24 @@
     (hidden, ntwo, normed, q, kcat, vcat, lse, ab, wqkv, wo, gains, w_full) = first_call(
         lengths, position_bias, tok, small, qkv_weight, out_weight.T, w
     )
-    gain_one, gain_two, router = gains[0], gains[1], gains[2 : 2 + experts].T.astype(BF)
-    f32dot = functools.partial(jnp.einsum, preferred_element_type=F32)
-    probs = jax.nn.softmax(f32dot("td,de->te", ntwo, router), axis=-1)
-    chosen = (expert_ids.reshape(rows)[:, None] == jnp.arange(experts)[None, :]).astype(F32)
-    gate = jnp.sum(probs * chosen, axis=-1)
-    positions = cx * seg + jnp.arange(seg, dtype=jnp.int32)
-    live = (positions[None, :] < lengths[:, None]).astype(F32).reshape(rows, 1)
-    upstream = live * cotangent.reshape(rows, width).astype(F32)
-    sum_grad = (gate[:, None] * upstream).astype(BF)
-    slots = slot_rows[:, 0]
-    place = jnp.where(slots < seg, slots + jnp.arange(micro)[:, None, None] * seg, rows)
-    place = jnp.transpose(place, (1, 0, 2)).reshape(experts, -1)
-    one_hot = (place[:, :, None] == jnp.arange(rows)[None, None, :]).astype(BF)
-    picked = f32dot("ekt,td->ekd", one_hot, ntwo).astype(BF)
-    slot_grad = f32dot("ekt,td->ekd", one_hot, sum_grad).astype(BF)
-    up, dn = w_full[:, 0], w_full[:, 1]
-    raised = f32dot("ekd,edf->ekf", picked, up)
-    activated, gelu_back = jax.vjp(jax.nn.gelu, raised)
-    activated = activated.astype(BF)
-    lowered = f32dot("ekf,edf->ekd", activated, dn).astype(BF)
-    spread = f32dot("ekt,ekd->td", one_hot, lowered).astype(BF)
-    down_part = f32dot("ekd,ekf->edf", slot_grad, activated)
-    act_grad = f32dot("ekd,edf->ekf", slot_grad, dn)
-    raised_grad = gelu_back(act_grad)[0].astype(BF)
-    up_part = f32dot("ekd,ekf->edf", picked, raised_grad)
-    picked_grad = f32dot("ekf,edf->ekd", raised_grad, up).astype(BF)
-    spread_grad = f32dot("ekt,ekd->td", one_hot, picked_grad).astype(BF)
-    expert_sum = lax.psum(spread, "tensor").astype(F32)
-    result = (live * (hidden + gate[:, None] * expert_sum)).astype(BF)
-    gate_grad = jnp.sum(expert_sum * upstream, axis=-1)
-    logit_grad = (probs * gate_grad[:, None] * (chosen - gate[:, None])).astype(BF)
-    router_part = f32dot("td,te->de", ntwo, logit_grad)
-    normed_two_grad = lax.psum(spread_grad, "tensor").astype(F32) + f32dot(
-        "te,de->td", logit_grad, router
+    slots = slot_rows[:, 0].reshape(micro * experts, -1)
+    result, input_part, w_grad, small_grad, tiny, dbias = second_call(
+        lengths, position_bias, expert_ids.reshape(rows, 1), slots, slots.T,
+        cotangent.reshape(rows, width), ntwo, q, kcat, vcat, lse, ab, wqkv, wo, gains, normed, tok,
+        hidden, w_full,
     )
-    unused, second_back = jax.vjp(rms_norm, hidden, gain_two)
-    hidden_grad, gain_two_part = second_back(normed_two_grad)
-    hidden_grad = hidden_grad + upstream
-    branch_grad = hidden_grad.astype(BF)
-    out_part = f32dot("td,te->de", branch_grad, ab)
-    attended_grad = f32dot("td,de->te", branch_grad, wo).astype(BF)
-    dq, dk, dv, dbias = back_call(lengths, position_bias, q, kcat, vcat, lse, attended_grad)
-    dkv = jnp.stack([dk * 0.125, dv], axis=0).astype(BF)
-    other = lax.dynamic_slice_in_dim(dkv, (1 - cx) * seg, seg, axis=2)
-    own = lax.dynamic_slice_in_dim(dkv, cx * seg, seg, axis=2)
-    came = lax.ppermute(other, "ctx", [(0, 1), (1, 0)])
-    own = (own.astype(F32) + came.astype(F32)).astype(BF).reshape(2, rows, -1)
-    grads = jnp.stack([dq, own[0], own[1]], axis=0)
-    qkv_part = f32dot("td,cte->dce", normed, grads)
-    normed_grad = lax.psum(f32dot("cte,cde->td", grads, wqkv).astype(BF), "tensor").astype(F32)
-    unused, first_back = jax.vjp(rms_norm, tok.astype(F32), gain_one)
-    token_grad, gain_one_part = first_back(normed_grad)
-    input_part = (token_grad + hidden_grad).astype(BF)
-    both = ("dp", "ctx")
-
-    def scatter(v, dim):
-        return lax.psum_scatter(v, both, scatter_dimension=dim, tiled=True)
-
-    up_grad = scatter(up_part.astype(BF), 1).astype(F32)
-    down_grad = jnp.transpose(scatter(down_part.astype(BF), 1).astype(F32), (0, 2, 1))
-    rest = scatter(
-        jnp.concatenate([qkv_part.reshape(width, -1), out_part], axis=1).astype(BF), 0
-    ).astype(F32)
-    span = q.shape[1]
-    qkv_grad = jnp.transpose(rest[:, : 3 * span].reshape(shard, 3, span), (1, 0, 2))
-    out_grad = rest[:, 3 * span :].T
-    tiny = scatter(
-        jnp.concatenate([gain_one_part[:, None], gain_two_part[:, None], router_part], axis=1), 0
-    )
-    bias_grad = lax.psum(dbias, both)[:, : position_bias.shape[1]]
+    tiny = lax.dynamic_slice_in_dim(tiny, slab * shard, shard, axis=1)
     return (
         result.reshape(inputs.shape),
         input_part.reshape(inputs.shape),
-        tiny[:, 0],
-        qkv_grad,
-        out_grad,
-        bias_grad,
-        tiny[:, 1],
-        tiny[:, 2:],
-        up_grad,
-        down_grad,
+        tiny[0],
+        small_grad[:3],
+        small_grad[3].T,
+        dbias[:, : position_bias.shape[1]],
+        tiny[1],
+        tiny[2 : 2 + experts].T,
+        w_grad[:, 0],
+        jnp.transpose(w_grad[:, 1], (0, 2, 1)),
     )
 
 

time: 759 us -> 396 us (0.52); the launches traced: 749 us -> 394 us
  waiting for transfers between devices: 368 us -> 0 us
  Pallas kernels: 184 us -> 374 us
  matrix products: 76.7 us -> 0 us
  blocking collectives: 37.1 us -> 0 us
  other arithmetic: 33.7 us -> 3.13 us
  local copies, waits for them, and re-layouts: 32.3 us -> 15.5 us
  between operations: 15 us -> 0.76 us
    reduce_scatter x2 -> x0, waiting for transfers between devices: 192 us -> none  [scatter(): return lax.psum_scatter(v, both, scatter_dimension=dim, tiled=True)]
    pallas_call x1, Pallas kernels: 21.3 us -> 211 us  [second_call(): pl.pallas_call(functools.partial(second_kernel, heads), out_shape=(sds((r...]
    psum x2 -> x0, waiting for transfers between devices: 101 us -> none  [the longest x1 67.1 us: body_fast(): expert_sum = lax.psum(spread, 'tensor').astype(F32)]
    dot_general x14 -> x0, matrix products: 73.9 us -> none  [the longest x1 11.8 us: body_fast(): spread = f32dot('ekt,ekd->td', one_hot, lowered).astype(BF)]
    unnamed x8 -> x0, waiting for transfers between devices: 60.9 us -> none
    psum x1 -> x0, blocking collectives: 37.1 us -> none  [body_fast(): bias_grad = lax.psum(dbias, both)[:, :position_bias.shape[1]]]
    ppermute x1 -> x0, waiting for transfers between devices: 14.5 us -> none  [body_fast(): came = lax.ppermute(other, 'ctx', [(0, 1), (1, 0)])]
    unnamed x64 -> x26, local copies, waits for them, and re-layouts: 20.6 us -> 7.68 us
  transfers between devices with their start and end apart: 7 -> 0, of which waited for: 6 -> 0; matrix products, arithmetic and copies ran while one was open for 6% -> 0% of each run, Pallas kernels for 0% -> 0%
where the time goes in v2:
time: 396 us; the launch traced here: 394 us
  Pallas kernels  374 us (94%)
  local copies, waits for them, and re-layouts  15.5 us (4%)
    pallas_call x1, Pallas kernels, second_call(): pl.pallas_call(functools.partial(second_kernel, heads), out_shape=(sds((r...  211 us
    pallas_call x1, Pallas kernels, first_call(): pl.pallas_call(functools.partial(first_kernel, heads), out_shape=(jax.Sha...  163 us

profile of v2, /device:TPU:0, one launch (start us, length us, event | category | flops | bytes accessed | tf_op | source)
XLA Modules:
  0.0 393.8 jit_solution(6068237703666037061)
XLA Ops:
  0.6 0.0 copy-start.5
  0.7 0.1 pad.5.clone
  0.7 0.8 maximum_maximum_fusion
  1.5 0.2 dynamic_update_slice.3.small
  1.7 0.0 copy-start.3
  1.7 1.4 copy.33.bias_ref
  3.1 2.4 pad_maximum_fusion.w
  5.4 0.0 copy-done.5
  5.4 0.7 copy.31
  6.2 0.0 copy-done.3
  6.2 163.1 %shard_map.204 = (f32[1024,768]{1,0:T(8,128)}, bf16[1024,768]{1,0:T(8,128)(2,1)}, bf16[1024,768]{1,0:T(8,128)(2,1)}, bf16[1024,192]{1,0:T(8,128)(2,1)}, bf16[2,1...) custom-call(s32[2]{0:T(128)} %len_ref.3, ...), custom_call_target="tpu_custom_call" | custom-call | tf_op jit(solution)/shard_map/pallas_call | solution.py:493
  169.3 0.0 copy-done.7
  169.3 0.0 copy-start.4
  169.3 0.8 copy.30
  170.1 0.0 copy-done.8
  170.1 1.0 copy.38
  171.2 0.0 copy-done.4
  171.2 211.3 %shard_map.205 = (bf16[1024,768]{1,0:T(8,128)(2,1)}, bf16[1024,768]{1,0:T(8,128)(2,1)}, f32[4,2,96,768]{3,2,1,0:T(8,128)}, f32[4,96,192]{2,1,0:T(8,128)}, f32[16,768]{1,0:T(8,128)}, /*index=5*/f32[32,128]{1,0:T(8,128)}) custom-call(s32[2]{0:T(128)} %len_ref.3, f32[32,3]{1,0:T(8,128)} %copy.33.bias_ref, s32[1024,1]{1,0:T(8,128)} %bitcast.36, ...), custom_call_target="tpu_custom_call" | custom-call | tf_op jit(solution)/shard_map/pallas_call | solution.py:1169
  382.5 0.0 copy-start.2
  382.5 0.0 copy-start.6
  382.5 0.0 copy-start.1
  382.5 3.3 slice_bitcast_fusion
  385.9 0.0 copy-done.2
  385.9 0.7 slice.25
  386.6 0.7 copy.35
  387.3 1.3 dynamic-slice_bitcast_fusion
  388.7 1.4 dynamic-slice_bitcast_fusion.1
  390.1 0.0 copy-done.6
  390.1 0.7 copy.36
  390.7 1.1 copy.42
  391.9 0.8 copy-done
  392.7 1.1 copy.43
  (9 shorter events, 0.0 us)
Async XLA Ops:
  0.6 4.8 %copy-start.5 = (bf16[192,96]{1,0:T(8,128)(2,1)S(1)}, bf16[192,96]{1,0:T(8,128)(2,1)}, u32[]{:S(2)}) copy-start(bf16[192,96]{1,0:T(8,128)(2,1)} %param.19) | copy-start | bytes 110596
  1.7 4.5 %copy-start.3 = (bf16[16,768]{1,0:T(8,128)(2,1)}, bf16[16,768]{1,0:T(8,128)(2,1)S(1)}, u32[]{:S(2)}) copy-start(bf16[16,768]{1,0:T(8,128)(2,1)S(1)} %dynamic_update_slice.3.small) | copy-start | bytes 73732
  5.4 163.8 %copy-start.7 = (s32[2,1,4,256]{3,2,1,0:T(4,128)S(1)}, s32[2,1,4,256]{3,2,1,0:T(4,128)}, u32[]{:S(2)}) copy-start(s32[2,1,4,256]{3,2,1,0:T(4,128)} %param.16) | copy-start | bytes 24580
  6.2 163.9 %copy-start.8 = (s32[2,512]{1,0:T(2,128)S(1)}, s32[2,512]{1,0:T(2,128)}, u32[]{:S(2)}) copy-start(s32[2,512]{1,0:T(2,128)} %param.15) | copy-start | bytes 12292
  169.3 1.8 copy-start.4
  382.5 3.4 copy-start.2
  382.5 7.5 %copy-start.6 = (f32[32,128]{1,0:T(8,128)S(1)}, f32[32,128]{1,0:T(8,128)}, u32[]{:S(2)}) copy-start(f32[32,128]{1,0:T(8,128)} %get-tuple-element.44) | copy-start | bytes 49156
  382.5 8.2 %copy-start.1 = (bf16[1024,768]{1,0:T(8,128)(2,1)S(1)}, bf16[1024,768]{1,0:T(8,128)(2,1)}, u32[]{:S(2)}) copy-start(bf16[1024,768]{1,0:T(8,128)(2,1)} %get-tuple-element.40) | copy-start | bytes 4718596
  390.7 2.0 copy-start

commit v3 on v0

--- a/solution.py
+++ b/solution.py
@@ -1,13 +1,1205 @@
+import functools
+
 import jax
 import jax.numpy as jnp
 import numpy as np
 from jax import lax
+from jax.experimental import pallas as pl
+from jax.experimental.pallas import tpu as pltpu
 from jax.sharding import PartitionSpec as P
 
 BUCKETS = 32
+MESH = pl.DeviceIdType.MESH
+BF = jnp.bfloat16
+F32 = jnp.float32
 
 
 bucket_edges = np.ceil(16.0 * 8.0 ** (np.arange(1, 16) / 16.0)).astype(np.int32)
+bucket_starts = [int(n) for n in range(17)] + [int(n) for n in bucket_edges]
+
+
+QT = 256
+BAND = 128
+C0 = float(np.sqrt(2.0 / np.pi))
+C1 = 0.044715
+
+
+def mm(a, b):
+    return jnp.dot(a, b, preferred_element_type=F32)
+
+
+def mm_nt(a, b):
+    return lax.dot_general(a, b, (((1,), (1,)), ((), ())), preferred_element_type=F32)
+
+
+def mm_tn(a, b):
+    return lax.dot_general(a, b, (((0,), (0,)), ((), ())), preferred_element_type=F32)
+
+
+def remote(src, dst, send, recv, device):
+    return pltpu.make_async_remote_copy(
+        src_ref=src,
+        dst_ref=dst,
+        send_sem=send,
+        recv_sem=recv,
+        device_id=device,
+        device_id_type=MESH,
+    )
+
+
+def block(start, size, whole=128):
+    return pl.ds(pl.multiple_of(start, whole), size)
+
+
+class Place:
+    def __init__(self):
+        dp, cx, t = lax.axis_index("dp"), lax.axis_index("ctx"), lax.axis_index("tensor")
+        self.dp, self.cx, self.t = dp, cx, t
+        self.yy, self.core = lax.div(t, 2), lax.rem(t, 2)
+        self.partner = (dp, 1 - cx, t)
+        self.sibling = (dp, cx, t + 1 - 2 * self.core)
+        self.across = (dp, cx, lax.rem(t + 2, 4))
+        self.tensor_peers = [(dp, cx, lax.rem(t + k, 4)) for k in (1, 2, 3)]
+        self.z_peers = [(lax.rem(dp + k, 4), cx, t) for k in (1, 2, 3)]
+        self.spot = dp + cx * (7 - 2 * dp)
+        self.right = self.at_spot(1)
+        self.left = self.at_spot(-1)
+
+    def at_spot(self, away):
+        spot = lax.rem(self.spot + 8 + away, 8)
+        cx = lax.div(spot, 4)
+        return (spot + cx * (7 - 2 * spot), cx, self.t)
+
+    def slab(self, away):
+        dp, cx, _ = self.at_spot(away)
+        return dp * 2 + cx
+
+    def greet(self):
+        barrier = pltpu.get_barrier_semaphore()
+        peers = self.z_peers + [self.partner] + self.tensor_peers
+        for peer in peers:
+            pl.semaphore_signal(barrier, inc=1, device_id=peer, device_id_type=MESH)
+        pl.semaphore_wait(barrier, len(peers))
+
+
+class Ring:
+    def __init__(self, place, send_sems, recv_sems):
+        self.place, self.send_sems, self.recv_sems = place, send_sems, recv_sems
+
+    def copy(self, d, e, s, src, dst):
+        at = (d, e, s - 1)
+        device = self.place.right if d == 0 else self.place.left
+        return remote(src, dst, self.send_sems.at[at], self.recv_sems.at[at], device)
+
+
+class TensorSum:
+    def __init__(self, place, seg, cbuf, ysend, ybuf, kept, c_s, c_r, y_s, y_r, a_s, a_r):
+        self.place, self.seg = place, seg
+        self.half, self.quarter = seg // 2, seg // 4
+        self.cbuf, self.ysend, self.ybuf, self.kept = cbuf, ysend, ybuf, kept
+        self.c_s, self.c_r, self.y_s, self.y_r, self.a_s, self.a_r = c_s, c_r, y_s, y_r, a_s, a_r
+
+    def rows(self, m, c, y):
+        return block(m * self.seg + c * self.half + y * self.quarter, self.quarter)
+
+    def own_rows(self, m):
+        return self.rows(m, self.place.core, self.place.yy)
+
+    def c_copy(self, m, j, src):
+        rows = block(m * self.seg + (1 - self.place.core) * self.half, self.half)
+        return remote(
+            src.at[rows], self.cbuf.at[m, j % 2], self.c_s.at[m, j], self.c_r.at[m, j],
+            self.place.sibling,
+        )
+
+    def y_copy(self, m, j):
+        return remote(
+            self.ysend.at[m, j % 2], self.ybuf.at[m, j % 2], self.y_s.at[m, j], self.y_r.at[m, j],
+            self.place.across,
+        )
+
+    def to_quarters(self, m, j, src):
+        self.c_copy(m, j, src).wait_recv()
+        yy, core = self.place.yy, self.place.core
+        near, far = block(yy * self.quarter, self.quarter), block((1 - yy) * self.quarter, self.quarter)
+        other = src[self.rows(m, core, 1 - yy), :].astype(F32)
+        self.ysend[m, j % 2] = (other + self.cbuf[m, j % 2, far, :].astype(F32)).astype(BF)
+        self.y_copy(m, j).start()
+        mine = src[self.rows(m, core, yy), :].astype(F32)
+        self.kept[m, j % 2] = mine + self.cbuf[m, j % 2, near, :].astype(F32)
+
+    def total(self, m, j):
+        self.y_copy(m, j).wait_recv()
+        return self.kept[m, j % 2] + self.ybuf[m, j % 2].astype(F32)
+
+    def a_copy(self, m, j, ref, step, own=None):
+        yy, core = self.place.yy, self.place.core
+        spot = ref.at[self.rows(m, core, 1 - yy if step == 2 else yy)]
+        source = spot if own is None or step == 2 else own
+        return remote(
+            source, spot, self.a_s.at[m, j, step], self.a_r.at[m, j, step],
+            self.place.across if step == 0 else self.place.sibling,
+        )
+
+    def a_recv(self, m, j, ref, step):
+        yy, core = self.place.yy, self.place.core
+        spot = ref.at[
+            self.rows(m, core if step == 0 else 1 - core, yy if step == 1 else 1 - yy)
+        ]
+        return remote(
+            spot, spot, self.a_s.at[m, j, step], self.a_r.at[m, j, step], self.place.sibling
+        )
+
+    def share(self, m, j, ref, own=None):
+        self.a_copy(m, j, ref, 0, own).start()
+        self.a_copy(m, j, ref, 1, own).start()
+
+    def pass_on(self, m, j, ref):
+        self.a_recv(m, j, ref, 0).wait_recv()
+        self.a_copy(m, j, ref, 2).start()
+
+    def shared(self, m, j, ref):
+        self.a_recv(m, j, ref, 1).wait_recv()
+        self.a_recv(m, j, ref, 2).wait_recv()
+
+
+def low_lanes(shape):
+    return lax.rem(lax.broadcasted_iota(jnp.int32, shape, len(shape) - 1), 128) < 64
+
+
+def head_lanes(h, base=0):
+    return slice(base + h * 128, base + (h + 1) * 128)
+
+
+def fill_bias(bias_ref, band_ref, heads):
+    rows = lax.broadcasted_iota(jnp.int32, (BAND, 2 * BAND), 0)
+    cols = lax.broadcasted_iota(jnp.int32, (BAND, 2 * BAND), 1)
+    away = rows + BAND - cols
+    for h in range(heads):
+        tile = jnp.full((BAND, 2 * BAND), bias_ref[0, h], F32)
+        for b in range(1, BUCKETS):
+            tile = jnp.where(away >= bucket_starts[b], bias_ref[b, h], tile)
+        band_ref[h] = tile - bias_ref[BUCKETS - 1, h]
+
+
+def masked_scores(q_tile, keys, band_ref, scores, h, first, length):
+    count = keys.shape[0]
+    scores[:, BAND:] = mm_nt(q_tile, keys) * 0.125
+    for part in range(QT // BAND):
+        spot = (block(part * BAND, BAND), block(first + part * BAND, 2 * BAND))
+        scores[spot] = scores[spot] + band_ref[h]
+    values = scores[:, BAND:]
+    key_pos = lax.broadcasted_iota(jnp.int32, (QT, count), 1)
+    query_pos = lax.broadcasted_iota(jnp.int32, (QT, count), 0) + first
+    allowed = (key_pos <= query_pos) & (key_pos < length)
+    return jnp.where(allowed, values, -1e30), allowed
+
+
+def bucket_sums(heads, band_sum, whole_sum, dbias):
+    rows = lax.broadcasted_iota(jnp.int32, (BAND, 2 * BAND), 0)
+    cols = lax.broadcasted_iota(jnp.int32, (BAND, 2 * BAND), 1)
+    away = rows + BAND - cols
+    bucket = lax.broadcasted_iota(jnp.int32, (BUCKETS, 2 * BAND), 0)
+    lanes128 = lax.broadcasted_iota(jnp.int32, (BUCKETS, 128), 1)
+    result = jnp.zeros((BUCKETS, 128), F32)
+    for h in range(heads):
+        tile = band_sum[h]
+        sums = jnp.zeros((BUCKETS, 2 * BAND), F32)
+        for b in range(BUCKETS - 1):
+            inside = (away >= bucket_starts[b]) & (away < bucket_starts[b + 1])
+            row = jnp.sum(jnp.where(inside, tile, 0.0), axis=0, keepdims=True)
+            sums = jnp.where(bucket == b, row, sums)
+        per_bucket = jnp.sum(sums, axis=1, keepdims=True)
+        near = jnp.sum(per_bucket, axis=0, keepdims=True)
+        total = jnp.sum(whole_sum[h : h + 1, :], axis=1, keepdims=True)
+        last = lax.broadcasted_iota(jnp.int32, (BUCKETS, 1), 0) == BUCKETS - 1
+        per_bucket = jnp.where(last, total - near, per_bucket)
+        result = jnp.where(lanes128 == h, per_bucket, result)
+    dbias[...] = result
+
+
+def norm_back(x, gain, grad):
+    scale = lax.rsqrt(jnp.mean(x * x, axis=-1, keepdims=True) + 1e-06)
+    unit = x * scale
+    pulled = grad * gain
+    inner = jnp.mean(pulled * unit, axis=-1, keepdims=True)
+    return scale * (pulled - unit * inner), grad * unit
+
+
+def first_kernel(
+    heads,
+    len_ref,
+    bias_ref,
+    tok,
+    wsmall,
+    w,
+    hidden,
+    ntwo,
+    normed,
+    q3,
+    kv,
+    lse,
+    ab3,
+    ws,
+    gains,
+    w_full,
+    ws_full,
+    bpart,
+    cbuf,
+    ysend,
+    ybuf,
+    kept,
+    band,
+    scores,
+    sz_s,
+    sz_r,
+    sx_s,
+    sx_r,
+    kv_s,
+    kv_r,
+    c_s,
+    c_r,
+    y_s,
+    y_r,
+    a_s,
+    a_r,
+    ring_s,
+    ring_r,
+    local,
+):
+    place = Place()
+    dp, cx, t = place.dp, place.cx, place.t
+    seg = tok.shape[0] // 2
+    width = tok.shape[1]
+    shard = width // 8
+    experts = w.shape[0]
+    span = kv.shape[2]
+    place.greet()
+    ring = Ring(place, ring_s, ring_r)
+    sums = TensorSum(place, seg, cbuf, ysend, ybuf, kept, c_s, c_r, y_s, y_r, a_s, a_r)
+
+    def small_slab(k, c):
+        return lax.rem(dp + 4 - k, 4) * 2 + c
+
+    def sz_copy(k, slab):
+        return remote(
+            wsmall, ws_full.at[slab], sz_s.at[k - 1], sz_r.at[k - 1], place.z_peers[k - 1]
+        )
+
+    def sx_copy(k, c):
+        spot = ws_full.at[small_slab(k, c)]
+        return remote(wsmall if k == 0 else spot, spot, sx_s.at[k], sx_r.at[k], place.partner)
+
+    small_own = pltpu.make_async_copy(wsmall, ws_full.at[small_slab(0, cx)], local.at[experts])
+
+    def gather(d, e, s, sending):
+        away = s - 1 if sending else s
+        slab = place.slab(-away if d == 0 else away)
+        if s == 4:
+            spot = w_full.at[e, d, slab]
+        else:
+            spot = w_full.at[e, :, slab]
+        return ring.copy(d, e, s, w.at[e] if sending and s == 1 else spot, spot)
+
+    def w_own(e):
+        return pltpu.make_async_copy(w.at[e], w_full.at[e, :, place.slab(0)], local.at[e])
+
+    steps = [(e, s) for s in (2, 3, 4) for e in range(experts)]
+
+    def pump(count=1):
+        for _ in range(count):
+            if steps:
+                e, s = steps.pop(0)
+                for d in range(2):
+                    gather(d, e, s - 1, False).wait_recv()
+                    gather(d, e, s, True).start()
+
+    small_own.start()
+    for k in (1, 3, 2):
+        sz_copy(k, small_slab(0, cx)).start()
+    sx_copy(0, cx).start()
+    for e in range(experts):
+        w_own(e).start()
+        for d in range(2):
+            gather(d, e, 1, True).start()
+
+    @pl.when(cx == 0)
+    def _():
+        for m in range(2):
+            kv[m, seg:, :] = jnp.zeros((seg, span), BF)
+
+    fill_bias(bias_ref, band, heads)
+    for k in (1, 3, 2):
+        sz_copy(k, small_slab(k, cx)).wait_recv()
+        sx_copy(k, cx).start()
+    small_own.wait()
+    for k in range(4):
+        sx_copy(k, 1 - cx).wait_recv()
+    total = ws_full[0, shard:, :].astype(F32)
+    for i in range(1, 8):
+        total = total + ws_full[i, shard:, :].astype(F32)
+    gains[...] = total
+    for i in range(8):
+        ws[i * shard : (i + 1) * shard, :] = ws_full[i, 0:shard, :]
+
+    def project(m):
+        def step(i, carry):
+            rows = block(m * seg + i * 256, 256)
+            x = tok[rows, :].astype(F32)
+            scale = lax.rsqrt(jnp.mean(x * x, axis=-1, keepdims=True) + 1e-06)
+            x = (x * scale * gains[0:1, :]).astype(BF)
+            normed[rows, :] = x
+            kv[m, block(cx * seg + i * 256, 256), :] = mm(x, ws[:, 0:span]).astype(BF)
+            part = mm(x, ws[:, span:])
+            q3[rows, :] = jnp.where(low_lanes(part.shape), part, 0.0).astype(BF)
+            return carry
+
+        lax.fori_loop(0, seg // 256, step, 0)
+
+    def kv_copy(m):
+        spot = kv.at[m, block(0, seg), :]
+        return remote(spot, spot, kv_s.at[m], kv_r.at[m], place.partner)
+
+    for m in range(2):
+        project(m)
+
+        @pl.when(cx == 0)
+        def _():
+            kv_copy(m).start()
+
+    pump(2)
+
+    def attend(m):
+        length = len_ref[m]
+
+        def step(i, carry):
+            rows = block(m * seg + i * QT, QT)
+            first = cx * seg + i * QT
+            lanes128 = lax.broadcasted_iota(jnp.int32, (QT, 128), 1)
+            tops = jnp.zeros((QT, 128), F32)
+            for h in range(heads):
+                cut = head_lanes(h)
+                values, allowed = masked_scores(
+                    q3[rows, cut], kv[m, :, cut], band, scores, h, first, length
+                )
+                top = jnp.max(values, axis=-1, keepdims=True)
+                raised = jnp.where(allowed, jnp.exp(values - top), 0.0)
+                mass = jnp.sum(raised, axis=-1, keepdims=True)
+                probs = (raised * (1.0 / mass)).astype(BF)
+                part = mm(probs, kv[m, :, cut])
+                ab3[rows, cut] = jnp.where(low_lanes(part.shape), 0.0, part).astype(BF)
+                tops = jnp.where(lanes128 == h, top + jnp.log(mass), tops)
+            lse[rows, :] = tops
+            bpart[rows, :] = mm_nt(ab3[rows, :], ws[:, span:]).astype(BF)
+            return carry
+
+        lax.fori_loop(0, seg // QT, step, 0)
+
+    def second_norm(m):
+        rows = sums.own_rows(m)
+        x = tok[rows, :].astype(F32) + sums.total(m, 0)
+        hidden[m] = x
+        scale = lax.rsqrt(jnp.mean(x * x, axis=-1, keepdims=True) + 1e-06)
+        ntwo[rows, :] = (x * scale * gains[1:2, :]).astype(BF)
+        sums.share(m, 0, ntwo)
+
+    for m in range(2):
+
+        @pl.when(cx == 1)
+        def _():
+            kv_copy(m).wait_recv()
+
+        attend(m)
+        sums.c_copy(m, 0, bpart).start()
+        pump()
+        sums.to_quarters(m, 0, bpart)
+        if m == 1:
+            sums.pass_on(0, 0, ntwo)
+        pump()
+        second_norm(m)
+    sums.pass_on(1, 0, ntwo)
+    for m in range(2):
+        sums.shared(m, 0, ntwo)
+    pump(len(steps))
+
+    for e in range(experts):
+        w_own(e).wait()
+        for d in range(2):
+            gather(d, e, 4, False).wait_recv()
+    for k in (1, 2, 3):
+        sz_copy(k, small_slab(0, cx)).wait_send()
+    for k in range(4):
+        sx_copy(k, cx).wait_send()
+    for e in range(experts):
+        for d in range(2):
+            for s in (1, 2, 3, 4):
+                gather(d, e, s, True).wait_send()
+    for m in range(2):
+        sums.c_copy(m, 0, bpart).wait_send()
+        sums.y_copy(m, 0).wait_send()
+        for step in range(3):
+            sums.a_copy(m, 0, ntwo, step).wait_send()
+
+        @pl.when(cx == 0)
+        def _():
+            kv_copy(m).wait_send()
+
+
+def first_call(lengths, bias, tok, wsmall, w):
+    heads = bias.shape[1]
+    rows, width = tok.shape
+    span = heads * 128
+    experts = w.shape[0]
+    ff = w.shape[3]
+    quarter = rows // 8
+    vm = pl.BlockSpec(memory_space=pltpu.VMEM)
+    sm = pl.BlockSpec(memory_space=pltpu.SMEM)
+    hbm = pl.BlockSpec(memory_space=pl.ANY)
+    dma = pltpu.SemaphoreType.DMA
+    sds = jax.ShapeDtypeStruct
+    return pl.pallas_call(
+        functools.partial(first_kernel, heads),
+        out_shape=(
+            sds((2, quarter, width), F32),
+            sds((rows, width), BF),
+            sds((rows, width), BF),
+            sds((rows, span), BF),
+            sds((2, rows, span), BF),
+            sds((rows, 128), F32),
+            sds((rows, span), BF),
+            sds((width, width), BF),
+            sds((16, width), F32),
+            sds((experts, 2, 8, width // 8, ff), BF),
+        ),
+        in_specs=[sm, sm, vm, hbm, hbm],
+        out_specs=(vm,) * 9 + (hbm,),
+        scratch_shapes=[
+            pltpu.VMEM((8,) + wsmall.shape, BF),
+            pltpu.VMEM((rows, width), BF),
+            pltpu.VMEM((2, 1, 2 * quarter, width), BF),
+            pltpu.VMEM((2, 1, quarter, width), BF),
+            pltpu.VMEM((2, 1, quarter, width), BF),
+            pltpu.VMEM((2, 1, quarter, width), F32),
+            pltpu.VMEM((heads, BAND, 2 * BAND), F32),
+            pltpu.VMEM((QT, rows + BAND), F32),
+            dma((3,)),
+            dma((3,)),
+            dma((4,)),
+            dma((4,)),
+            dma((2,)),
+            dma((2,)),
+            dma((2, 1)),
+            dma((2, 1)),
+            dma((2, 1)),
+            dma((2, 1)),
+            dma((2, 1, 3)),
+            dma((2, 1, 3)),
+            dma((2, experts, 4)),
+            dma((2, experts, 4)),
+            dma((experts + 1,)),
+        ],
+        compiler_params=pltpu.CompilerParams(
+            collective_id=0, has_side_effects=True, vmem_limit_bytes=56 << 20
+        ),
+    )(lengths, bias, tok, wsmall, w)
+
+
+def second_kernel(
+    heads,
+    len_ref,
+    bias_ref,
+    ids,
+    slot_lanes,
+    slot_subs,
+    cot,
+    ntwo,
+    q3,
+    kv,
+    lse,
+    ab3,
+    ws,
+    gains,
+    hidden,
+    normed_hbm,
+    tok_hbm,
+    w_full,
+    result,
+    input_grad,
+    w_grad,
+    small_grad,
+    tiny_out,
+    dbias_out,
+    wbuf,
+    gw,
+    first_in,
+    second_in,
+    gs,
+    sx,
+    sz,
+    sum_grad,
+    epart,
+    npart,
+    ffn,
+    probs_ref,
+    tok,
+    cbuf,
+    ysend,
+    ybuf,
+    kept,
+    hgrad,
+    bgrad,
+    own_out,
+    do3,
+    grads,
+    dkv_acc,
+    dkv,
+    band,
+    scores,
+    spread,
+    band_sum,
+    whole_sum,
+    tiny_own,
+    tiny_t,
+    tiny_x,
+    tiny_z,
+    dbias_own,
+    dbias_x,
+    dbias_z,
+    load_sem,
+    row_sem,
+    out_sem,
+    ready,
+    ring_s,
+    ring_r,
+    c_s,
+    c_r,
+    y_s,
+    y_r,
+    a_s,
+    a_r,
+    kv_s,
+    kv_r,
+    sx_s,
+    sx_r,
+    sz_s,
+    sz_r,
+    tt_s,
+    tt_r,
+    tx_s,
+    tx_r,
+    tz_s,
+    tz_r,
+    bx_s,
+    bx_r,
+    bz_s,
+    bz_r,
+):
+    place = Place()
+    dp, cx, t = place.dp, place.cx, place.t
+    seg = cot.shape[0] // 2
+    width = cot.shape[1]
+    shard = width // 8
+    span = kv.shape[2]
+    experts = w_full.shape[0]
+    cap = slot_subs.shape[0]
+    place.greet()
+    ring = Ring(place, ring_s, ring_r)
+    sums = TensorSum(place, seg, cbuf, ysend, ybuf, kept, c_s, c_r, y_s, y_r, a_s, a_r)
+
+    def load(e, slot):
+        return pltpu.make_async_copy(w_full.at[e], wbuf.at[pl.ds(slot * 2, 2)], load_sem.at[slot])
+
+    def fetch(m):
+        return pltpu.make_async_copy(tok_hbm.at[sums.own_rows(m)], tok.at[m], row_sem.at[m])
+
+    load(0, 0).start()
+    for m in range(2):
+        fetch(m).start()
+
+    router16 = gains[...].astype(BF)
+
+    def upstream_of(rows, m, first):
+        spot = lax.broadcasted_iota(jnp.int32, (rows.size, 1), 0) + (cx * seg + first)
+        live = (spot < len_ref[m]).astype(F32)
+        return live, live * cot[rows, :].astype(F32)
+
+    def chosen_of(rows):
+        lanes = lax.broadcasted_iota(jnp.int32, (rows.size, 16), 1)
+        return (lanes == ids[rows, :] + 2).astype(F32)
+
+    for m in range(2):
+
+        def gates(i, carry):
+            rows = block(m * seg + i * 256, 256)
+            logits = mm_nt(ntwo[rows, :], router16)
+            lanes = lax.broadcasted_iota(jnp.int32, (256, 16), 1)
+            inside = (lanes >= 2) & (lanes < 2 + experts)
+            logits = jnp.where(inside, logits, -1e30)
+            top = jnp.max(logits, axis=-1, keepdims=True)
+            raised = jnp.where(inside, jnp.exp(logits - top), 0.0)
+            probs = raised / jnp.sum(raised, axis=-1, keepdims=True)
+            probs_ref[rows, :] = probs
+            gate = jnp.sum(probs * chosen_of(rows), axis=-1, keepdims=True)
+            live, upstream = upstream_of(rows, m, i * 256)
+            sum_grad[rows, :] = (gate * upstream).astype(BF)
+            epart[rows, :] = jnp.zeros((256, width), BF)
+            npart[rows, :] = jnp.zeros((256, width), BF)
+            return carry
+
+        lax.fori_loop(0, seg // 256, gates, 0)
+
+    def landing(d, e, s):
+        if s == 1:
+            return first_in.at[d, e]
+        if s == 2:
+            return second_in.at[d, e]
+        return wbuf.at[e, pl.ds(d * 4 + (s - 3) * 2, 2)]
+
+    def reduce_copy(d, e, s):
+        slab = place.slab(5 - s if d == 0 else s - 5)
+        src = gw.at[e, d, slab] if s == 1 else gw.at[e, :, slab]
+        return ring.copy(d, e, s, src, landing(d, e, s))
+
+    def reduce_first(e):
+        for d in range(2):
+            reduce_copy(d, e, 1).start()
+
+    def reduce_step(e, s):
+        for d in range(2):
+            slab = place.slab(5 - s if d == 0 else s - 5)
+            reduce_copy(d, e, s - 1).wait_recv()
+            came = landing(d, e, s - 1)[...].astype(F32)
+            if s == 2:
+                gw[e, d, slab] = (gw[e, d, slab].astype(F32) + came).astype(BF)
+            else:
+                gw[e, :, slab] = (gw[e, :, slab].astype(F32) + came).astype(BF)
+            reduce_copy(d, e, s).start()
+
+    def reduce_end(e):
+        total = gw[e, :, place.slab(0)].astype(F32)
+        for d in range(2):
+            reduce_copy(d, e, 4).wait_recv()
+            total = total + landing(d, e, 4)[...].astype(F32)
+        w_grad[e] = total
+
+    steps = [(experts - 1, 2)] + [(e, s) for s in (3, 4) for e in range(experts)]
+
+    def pump(count=1):
+        for _ in range(count):
+            if steps:
+                reduce_step(*steps.pop(0))
+
+    def weight(slot, which):
+        return wbuf[slot * 2 + which].reshape(width, -1)
+
+    picked, slot_grad, activated, raised_grad = (ffn.at[i] for i in range(4))
+
+    def expert_step(e, carry):
+        slot = lax.rem(e, 2)
+        load(e, slot).wait()
+
+        @pl.when(e + 1 < experts)
+        def _():
+            load(e + 1, 1 - slot).start()
+
+        def one_micro(m, carry):
+            rows = block(m * seg, seg)
+            slots = block(m * cap, cap)
+            lanes = lax.broadcasted_iota(jnp.int32, (cap, 8), 1)
+            column = jnp.sum(
+                jnp.where(lanes == m * experts + e, slot_subs[...], 0), axis=1, keepdims=True
+            )
+            pick = (column == lax.broadcasted_iota(jnp.int32, (cap, seg), 1)).astype(BF)
+            row = slot_lanes[pl.ds(m * experts + e, 1), :]
+            put = (row == lax.broadcasted_iota(jnp.int32, (seg, cap), 0)).astype(BF)
+            chosen_rows = mm(pick, ntwo[rows, :]).astype(BF)
+            picked[slots, :] = chosen_rows
+            slot_part = mm(pick, sum_grad[rows, :]).astype(BF)
+            slot_grad[slots, :] = slot_part
+            raised = mm(chosen_rows, weight(slot, 0))
+            square = raised * raised
+            bent = jnp.tanh(C0 * raised * (1.0 + C1 * square))
+            cdf = 0.5 * (1.0 + bent)
+            act = (raised * cdf).astype(BF)
+            activated[slots, :] = act
+            slope = cdf + 0.5 * raised * (1.0 - bent * bent) * (C0 * (1.0 + 3.0 * C1 * square))
+            act_grad = mm(slot_part, weight(slot, 1))
+            back = (act_grad * slope).astype(BF)
+            raised_grad[slots, :] = back
+            lowered = mm_nt(act, weight(slot, 1)).astype(BF)
+            epart[rows, :] += mm(put, lowered).astype(BF)
+            pulled = mm_nt(back, weight(slot, 0)).astype(BF)
+            npart[rows, :] += mm(put, pulled).astype(BF)
+            return carry
+
+        lax.fori_loop(0, 2, one_micro, 0)
+
+        def weight_part(i, carry):
+            lanes = block(i * 384, 384)
+            slabs = pl.ds(i * 4, 4)
+            part = mm_tn(picked[:, lanes], raised_grad[...]).astype(BF)
+            gw[e, 0, slabs] = part.reshape(4, shard, -1)
+            part = mm_tn(slot_grad[:, lanes], activated[...]).astype(BF)
+            gw[e, 1, slabs] = part.reshape(4, shard, -1)
+            return carry
+
+        lax.fori_loop(0, width // 384, weight_part, 0)
+        reduce_first(e)
+
+        @pl.when(e > 0)
+        def _():
+            reduce_step(e - 1, 2)
+
+        return carry
+
+    lax.fori_loop(0, experts, expert_step, 0)
+
+    for peer in (place.right, place.left):
+        pl.semaphore_signal(ready, inc=1, device_id=peer, device_id_type=MESH)
+
+    parts = (epart, npart)
+    for m in range(2):
+        for j in range(2):
+            sums.c_copy(m, j, parts[j]).start()
+
+    def fetch_normed(i):
+        return pltpu.make_async_copy(normed_hbm.at[pl.ds(i * seg, seg)], ffn.at[i], load_sem.at[i])
+
+    fetch_normed(0).start()
+    fetch_normed(1).start()
+    for m in range(2):
+        for j in range(2):
+            sums.to_quarters(m, j, parts[j])
+    pump()
+    fill_bias(bias_ref, band, heads)
+    spread[...] = jnp.zeros(spread.shape, F32)
+    band_sum[...] = jnp.zeros(band_sum.shape, F32)
+    whole_sum[...] = jnp.zeros(whole_sum.shape, F32)
+    tiny_own[...] = jnp.zeros(tiny_own.shape, F32)
+    pl.semaphore_wait(ready, 2)
+    pump()
+
+    def own_copy(m, j, ref):
+        return pltpu.make_async_copy(
+            own_out.at[m, j - 1], ref.at[sums.own_rows(m)], out_sem.at[m * 2 + j - 1]
+        )
+
+    for m in range(2):
+        rows = sums.own_rows(m)
+        expert_sum, down = sums.total(m, 0), sums.total(m, 1)
+        first = place.core * (seg // 2) + place.yy * (seg // 4)
+        live, upstream = upstream_of(rows, m, first)
+        probs, chosen = probs_ref[rows, :], chosen_of(rows)
+        gate = jnp.sum(probs * chosen, axis=-1, keepdims=True)
+        gate_grad = jnp.sum(expert_sum * upstream, axis=-1, keepdims=True)
+        logit_grad = (probs * gate_grad * (chosen - gate)).astype(BF)
+        x = hidden[m]
+        down = down + mm(logit_grad, router16)
+        through, gain_terms = norm_back(x, gains[1:2, :], down)
+        full = through + upstream
+        hgrad[m] = full
+        bgrad[rows, :] = full.astype(BF)
+        sums.share(m, 0, bgrad)
+        own_out[m, 0] = (live * (x + gate * expert_sum)).astype(BF)
+        own_copy(m, 1, result).start()
+        tiny_own[1:2, :] += jnp.sum(gain_terms, axis=0, keepdims=True)
+        tiny_own[...] += mm_tn(logit_grad, ntwo[rows, :])[0:8, :]
+    pump()
+    for m in range(2):
+        sums.pass_on(m, 0, bgrad)
+    for m in range(2):
+        sums.share(m, 1, result, own_out.at[m, 0])
+
+    def dkv_copy(m, h):
+        spot = dkv.at[m, h]
+        return remote(spot, spot, kv_s.at[m, h], kv_r.at[m, h], place.partner)
+
+    def attend_back(m):
+        length = len_ref[m]
+
+        def lower(i, carry):
+            part = mm(bgrad[block(m * seg + i * 256, 256), :], ws[:, span:])
+            part = jnp.where(low_lanes(part.shape), 0.0, part)
+            do3[block(i * 256, 256), :] = part.astype(BF)
+            return carry
+
+        lax.fori_loop(0, seg // 256, lower, 0)
+        for h in range(heads):
+            cut = head_lanes(h)
+            dkv_acc[...] = jnp.zeros(dkv_acc.shape, F32)
+
+            def step(i, carry):
+                rows = block(m * seg + i * QT, QT)
+                first = cx * seg + i * QT
+                q_tile, do_tile = q3[rows, cut], do3[block(i * QT, QT), cut]
+                keys = kv[m, :, cut]
+                values, allowed = masked_scores(q_tile, keys, band, scores, h, first, length)
+                soft = jnp.where(allowed, jnp.exp(values - lse[rows, h : h + 1]), 0.0)
+                soft_grad = mm_nt(do_tile, keys)
+                delta = jnp.sum(soft * soft_grad, axis=-1, keepdims=True)
+                score_grad = (soft * (soft_grad - delta)).astype(BF)
+                dkv_acc[...] += mm_tn(soft.astype(BF), do_tile) + 0.125 * mm_tn(score_grad, q_tile)
+                part = mm(score_grad, keys) * 0.125
+                grads[rows, head_lanes(h, span)] = jnp.where(
+                    low_lanes(part.shape), part, 0.0
+                ).astype(BF)
+                spread[:, BAND:] = score_grad.astype(F32)
+                for part in range(QT // BAND):
+                    lanes = block(first + part * BAND, 2 * BAND)
+                    band_sum[h] += spread[part * BAND : (part + 1) * BAND, lanes]
+                whole_sum[h : h + 1, :] += jnp.sum(spread[:, BAND:], axis=0, keepdims=True)
+                return carry
+
+            lax.fori_loop(0, seg // QT, step, 0)
+
+            @pl.when(cx == 1)
+            def _():
+                dkv[m, h] = dkv_acc[0:seg, :].astype(BF)
+                dkv_copy(m, h).start()
+
+            grads[pl.ds(m * seg, seg), cut] = dkv_acc[block(cx * seg, seg), :].astype(BF)
+            if h % 2 == 1:
+                pump()
+
+    def after_attend(m):
+        rows = pl.ds(m * seg, seg)
+
+        @pl.when(cx == 0)
+        def _():
+            for h in range(heads):
+                dkv_copy(m, h).wait_recv()
+                total = grads[rows, head_lanes(h)].astype(F32) + dkv[m, h].astype(F32)
+                grads[rows, head_lanes(h)] = total.astype(BF)
+
+        def lower(i, carry):
+            spot = block(m * seg + i * 256, 256)
+            npart[spot, :] = mm_nt(grads[spot, :], ws[...]).astype(BF)
+            return carry
+
+        lax.fori_loop(0, seg // 256, lower, 0)
+        sums.c_copy(m, 2, npart).start()
+
+    for m in range(2):
+        sums.shared(m, 0, bgrad)
+        attend_back(m)
+        if m == 1:
+            sums.c_copy(0, 1, npart).wait_send()
+            sums.y_copy(0, 0).wait_send()
+            after_attend(0)
+    sums.c_copy(1, 1, npart).wait_send()
+    sums.y_copy(1, 0).wait_send()
+    sums.to_quarters(0, 2, npart)
+    for m in range(2):
+        sums.pass_on(m, 1, result)
+
+    bucket_sums(heads, band_sum, whole_sum, dbias_own)
+    bx_copy = remote(dbias_own, dbias_x, bx_s.at[0], bx_r.at[0], place.partner)
+    bx_copy.start()
+
+    def out_part(i, carry):
+        lanes = block(i * 256, 256)
+        gs[lanes, span:] = mm_tn(bgrad[:, lanes], ab3[...]).astype(BF)
+        return carry
+
+    lax.fori_loop(0, width // 256, out_part, 0)
+    after_attend(1)
+    bx_copy.wait_recv()
+    dbias_own_sum = dbias_own[...] + dbias_x[...]
+    dbias_out[...] = dbias_own_sum
+
+    def bz_copy(k):
+        return remote(
+            dbias_out, dbias_z.at[k - 1], bz_s.at[k - 1], bz_r.at[k - 1], place.z_peers[k - 1]
+        )
+
+    for k in (1, 2, 3):
+        bz_copy(k).start()
+    fetch_normed(0).wait()
+    fetch_normed(1).wait()
+
+    def qkv_part(i, carry):
+        lanes = block(i * 256, 256)
+        part = mm_tn(ffn[0, :, lanes], grads[0:seg, :])
+        part = part + mm_tn(ffn[1, :, lanes], grads[seg:, :])
+        gs[lanes, 0:span] = part[:, 0:span].astype(BF)
+        both = part[:, span:] + gs[lanes, span:].astype(F32)
+        gs[lanes, span:] = both.astype(BF)
+        return carry
+
+    lax.fori_loop(0, width // 256, qkv_part, 0)
+    sums.to_quarters(1, 2, npart)
+
+    def slab_rows(d, c):
+        return block(d * 2 * shard + c * shard, shard, 32)
+
+    def sx_copy(k):
+        rows = slab_rows(lax.rem(dp + k, 4), 1 - cx)
+        return remote(gs.at[rows, :], sx.at[k], sx_s.at[k], sx_r.at[k], place.partner)
+
+    def sz_copy(k):
+        return remote(sx.at[k], sz.at[k - 1], sz_s.at[k - 1], sz_r.at[k - 1], place.z_peers[k - 1])
+
+    order = (2, 1, 3, 0)
+    for k in order:
+        sx_copy(k).start()
+
+    for m in range(2):
+        down = sums.total(m, 2)
+        fetch(m).wait()
+        through, gain_terms = norm_back(tok[m].astype(F32), gains[0:1, :], down)
+        own_out[m, 1] = (through + hgrad[m]).astype(BF)
+        sums.share(m, 2, input_grad, own_out.at[m, 1])
+        own_copy(m, 2, input_grad).start()
+        tiny_own[0:1, :] += jnp.sum(gain_terms, axis=0, keepdims=True)
+
+    def tt_copy(k):
+        return remote(
+            tiny_own, tiny_t.at[k - 1], tt_s.at[k - 1], tt_r.at[k - 1], place.tensor_peers[k - 1]
+        )
+
+    for k in (1, 2, 3):
+        tt_copy(k).start()
+    pump(len(steps))
+    for k in order:
+        sx_copy(k).wait_recv()
+        rows = slab_rows(lax.rem(dp + k, 4), cx)
+        total = gs[rows, :].astype(F32) + sx[k].astype(F32)
+        if k == 0:
+            small_grad[...] = total
+        else:
+            sx[k] = total.astype(BF)
+            sz_copy(k).start()
+
+    for k in (1, 2, 3):
+        tt_copy(k).wait_recv()
+    tiny_x[0] = tiny_own[...] + tiny_t[0] + tiny_t[1] + tiny_t[2]
+    tx_copy = remote(tiny_x.at[0], tiny_x.at[1], tx_s.at[0], tx_r.at[0], place.partner)
+    tx_copy.start()
+    for m in range(2):
+        sums.pass_on(m, 2, input_grad)
+    for e in range(experts):
+        reduce_end(e)
+    tx_copy.wait_recv()
+    tiny_x[2] = tiny_x[0] + tiny_x[1]
+
+    def tz_copy(k):
+        return remote(
+            tiny_x.at[2], tiny_z.at[k - 1], tz_s.at[k - 1], tz_r.at[k - 1], place.z_peers[k - 1]
+        )
+
+    for k in (1, 2, 3):
+        tz_copy(k).start()
+    total = small_grad[...]
+    for k in (1, 2, 3):
+        sz_copy(k).wait_recv()
+        total = total + sz[k - 1].astype(F32)
+    small_grad[...] = total
+    total = dbias_own_sum
+    for k in (1, 2, 3):
+        bz_copy(k).wait_recv()
+        total = total + dbias_z[k - 1]
+    for k in (1, 2, 3):
+        bz_copy(k).wait_send()
+    dbias_out[...] = total
+    total = tiny_x[2]
+    for k in (1, 2, 3):
+        tz_copy(k).wait_recv()
+        total = total + tiny_z[k - 1]
+    tiny_out[...] = total
+    for m in range(2):
+        sums.shared(m, 1, result)
+        sums.shared(m, 2, input_grad)
+
+    for e in range(experts):
+        for d in range(2):
+            for s in (1, 2, 3, 4):
+                reduce_copy(d, e, s).wait_send()
+    for k in range(4):
+        sx_copy(k).wait_send()
+        if k > 0:
+            sz_copy(k).wait_send()
+            tt_copy(k).wait_send()
+            tz_copy(k).wait_send()
+    tx_copy.wait_send()
+    bx_copy.wait_send()
+    for m in range(2):
+        sums.c_copy(m, 0, epart).wait_send()
+        sums.c_copy(m, 2, npart).wait_send()
+        own_copy(m, 1, result).wait()
+        own_copy(m, 2, input_grad).wait()
+        for j in range(3):
+            if j > 0:
+                sums.y_copy(m, j).wait_send()
+            for step in range(3):
+                own = None if j == 0 else own_out.at[m, j - 1]
+                sums.a_copy(m, j, (bgrad, result, input_grad)[j], step, own).wait_send()
+
+        @pl.when(cx == 1)
+        def _():
+            for h in range(heads):
+                dkv_copy(m, h).wait_send()
+
+
+def second_call(
+    lengths, bias, ids, slot_lanes, slot_subs, cot, ntwo, q3, kv, lse, ab3, ws, gains, hidden,
+    normed, tok, w_full,
+):
+    heads = bias.shape[1]
+    rows, width = cot.shape
+    span = q3.shape[1]
+    experts, ff = w_full.shape[0], w_full.shape[4]
+    seg = rows // 2
+    quarter = seg // 4
+    shard = width // 8
+    slots = 2 * slot_subs.shape[0]
+    vm = pl.BlockSpec(memory_space=pltpu.VMEM)
+    sm = pl.BlockSpec(memory_space=pltpu.SMEM)
+    hbm = pl.BlockSpec(memory_space=pl.ANY)
+    dma = pltpu.SemaphoreType.DMA
+    sds = jax.ShapeDtypeStruct
+    return pl.pallas_call(
+        functools.partial(second_kernel, heads),
+        out_shape=(
+            sds((rows, width), BF),
+            sds((rows, width), BF),
+            sds((experts, 2, shard, ff), F32),
+            sds((shard, width), F32),
+            sds((8, width), F32),
+            sds((BUCKETS, 128), F32),
+        ),
+        in_specs=[sm, sm] + [vm] * 12 + [hbm] * 3,
+        out_specs=(hbm,) * 2 + (vm,) * 4,
+        scratch_shapes=[
+            pltpu.VMEM((4, 8, shard, ff), BF),
+            pltpu.VMEM((experts, 2, 8, shard, ff), BF),
+            pltpu.VMEM((2, experts, shard, ff), BF),
+            pltpu.VMEM((2, experts, 2, shard, ff), BF),
+            pltpu.VMEM((width, width), BF),
+            pltpu.VMEM((4, shard, width), BF),
+            pltpu.VMEM((3, shard, width), BF),
+            pltpu.VMEM((rows, width), BF),
+            pltpu.VMEM((rows, width), BF),
+            pltpu.VMEM((rows, width), BF),
+            pltpu.VMEM((4, slots, width), BF),
+            pltpu.VMEM((rows, 16), F32),
+            pltpu.VMEM((2, quarter, width), BF),
+            pltpu.VMEM((2, 2, 2 * quarter, width), BF),
+            pltpu.VMEM((2, 2, quarter, width), BF),
+            pltpu.VMEM((2, 2, quarter, width), BF),
+            pltpu.VMEM((2, 2, quarter, width), F32),
+            pltpu.VMEM((2, quarter, width), F32),
+            pltpu.VMEM((rows, width), BF),
+            pltpu.VMEM((2, 2, quarter, width), BF),
+            pltpu.VMEM((seg, span), BF),
+            pltpu.VMEM((rows, 2 * span), BF),
+            pltpu.VMEM((rows, 128), F32),
+            pltpu.VMEM((2, heads, seg, 128), BF),
+            pltpu.VMEM((heads, BAND, 2 * BAND), F32),
+            pltpu.VMEM((QT, rows + BAND), F32),
+            pltpu.VMEM((QT, rows + BAND), F32),
+            pltpu.VMEM((heads, BAND, 2 * BAND), F32),
+            pltpu.VMEM((8, rows), F32),
+            pltpu.VMEM((8, width), F32),
+            pltpu.VMEM((3, 8, width), F32),
+            pltpu.VMEM((3, 8, width), F32),
+            pltpu.VMEM((3, 8, width), F32),
+            pltpu.VMEM((BUCKETS, 128), F32),
+            pltpu.VMEM((BUCKETS, 128), F32),
+            pltpu.VMEM((3, BUCKETS, 128), F32),
+            dma((2,)),
+            dma((2,)),
+            dma((4,)),
+            pltpu.SemaphoreType.REGULAR,
+            dma((2, experts, 4)),
+            dma((2, experts, 4)),
+            dma((2, 3)),
+            dma((2, 3)),
+            dma((2, 3)),
+            dma((2, 3)),
+            dma((2, 3, 3)),
+            dma((2, 3, 3)),
+            dma((2, heads)),
+            dma((2, heads)),
+            dma((4,)),
+            dma((4,)),
+        ]
+        + [dma((3,))] * 4
+        + [dma((1,))] * 2
+        + [dma((3,))] * 2
+        + [dma((1,))] * 2
+        + [dma((3,))] * 2,
+        compiler_params=pltpu.CompilerParams(
+            collective_id=1, has_side_effects=True, vmem_limit_bytes=63 << 20
+        ),
+    )(
+        lengths, bias, ids, slot_lanes, slot_subs, cot, ntwo, q3, kv, lse, ab3, ws, gains, hidden,
+        normed, tok, w_full,
+    )
+
+
+def body_fast(
+    inputs, lengths, expert_ids, slot_rows, attn_gain, qkv_weight, out_weight, position_bias,
+    ffn_gain, router_weight, up_weight, down_weight, cotangent,
+):
+    micro, seg, width = inputs.shape
+    rows = micro * seg
+    experts = up_weight.shape[0]
+    heads = position_bias.shape[1]
+    size = qkv_weight.shape[2] // heads
+    slab = lax.axis_index("dp") * 2 + lax.axis_index("ctx")
+    shard = attn_gain.shape[0]
+    by_head = jnp.concatenate(
+        [
+            qkv_weight[1].reshape(shard, heads, 1, size),
+            qkv_weight[2].reshape(shard, heads, 1, size),
+        ],
+        axis=2,
+    ).reshape(shard, -1)
+    by_query = jnp.concatenate(
+        [
+            qkv_weight[0].reshape(shard, heads, 1, size),
+            out_weight.T.reshape(shard, heads, 1, size),
+        ],
+        axis=2,
+    ).reshape(shard, -1)
+    small = jnp.concatenate(
+        [attn_gain[None], ffn_gain[None], router_weight.T, jnp.zeros((10, shard), BF)], axis=0
+    )
+    small = lax.dynamic_update_slice(jnp.zeros((16, width), BF), small, (0, slab * shard))
+    wsmall = jnp.concatenate([jnp.concatenate([by_head, by_query], axis=1), small], axis=0)
+    w = jnp.stack([up_weight, jnp.transpose(down_weight, (0, 2, 1))], axis=1)
+    tok = inputs.reshape(rows, width)
+    hidden, ntwo, normed, q3, kv, lse, ab3, ws, gains, w_full = first_call(
+        lengths, position_bias, tok, wsmall, w
+    )
+    slots = slot_rows[:, 0].reshape(micro * experts, -1)
+    result, input_part, w_grad, small_grad, tiny, dbias = second_call(
+        lengths, position_bias, expert_ids.reshape(rows, 1), slots, slots.T,
+        cotangent.reshape(rows, width), ntwo, q3, kv, lse, ab3, ws, gains, hidden, normed, tok, w_full,
+    )
+    tiny = lax.dynamic_slice_in_dim(tiny, slab * shard, shard, axis=1)
+    parts = small_grad.reshape(shard, 2, heads, 2, size)
+    qkv_grad = jnp.stack(
+        [parts[:, 1, :, 0], parts[:, 0, :, 0], parts[:, 0, :, 1]], axis=0
+    ).reshape(3, shard, heads * size)
+    return (
+        result.reshape(inputs.shape),
+        input_part.reshape(inputs.shape),
+        tiny[0],
+        qkv_grad,
+        parts[:, 1, :, 1].reshape(shard, heads * size).T,
+        dbias[:, :heads],
+        tiny[1],
+        tiny[2 : 2 + experts].T,
+        w_grad[:, 0],
+        jnp.transpose(w_grad[:, 1], (0, 2, 1)),
+    )
+
+
+def rms_norm(values, gain_vector):
+    return (
+        values * lax.rsqrt(jnp.mean(values * values, axis=-1, keepdims=True) + 1e-06) * gain_vector
+    )
 
 
 def bucket_of(distance):
@@ -15,12 +1207,6 @@
     edge_values = jnp.asarray(bucket_edges, dtype=jnp.int32)
     beyond = jnp.sum((clipped[..., None] >= edge_values).astype(jnp.int32), axis=-1)
     return jnp.where(clipped < 16, clipped, jnp.minimum(16 + beyond, 31))
-
-
-def rms_norm(values, gain_vector):
-    return (
-        values * lax.rsqrt(jnp.mean(values * values, axis=-1, keepdims=True) + 1e-06) * gain_vector
-    )
 
 
 def toeplitz(diagonal, query_count, key_count):
@@ -406,8 +1592,9 @@
 
 
 def solution(mesh):
+    small = mesh.shape["ctx"] == 2 and mesh.shape["dp"] == 4 and mesh.shape["tensor"] == 4
     return jax.shard_map(
-        body,
+        body_fast if small else body,
         mesh=mesh,
         in_specs=(
             P("dp", "ctx", None),

time: 1250 us -> 310 us (0.25); the launches traced: 1230 us -> 310 us
  waiting for transfers between devices: 438 us -> 0 us
  local copies, waits for them, and re-layouts: 390 us -> 17.3 us
  Pallas kernels: 0 us -> 288 us
  blocking collectives: 173 us -> 0 us
  matrix products: 120 us -> 0 us
  other arithmetic: 92.6 us -> 3.54 us
  between operations: 18.6 us -> 0.78 us
    pallas_call x0 -> x2, Pallas kernels: none -> 288 us  [the longest x1 154 us: second_call(): pl.pallas_call(functools.partial(second_kernel, heads), out_shape=(sds((r...]
    reduce_scatter x4 -> x0, waiting for transfers between devices: 264 us -> none  [the longest x1 166 us: body(): lax.psum_scatter(grad_sums[5], ('dp', 'ctx'), scatter_dimension=1, tiled=...]
    rev x3 -> x0, local copies, waits for them, and re-layouts: 147 us -> none  [the longest x2 96.3 us: diagonal_sums(): flipped = jnp.pad(gradient[:, :, ::-1], ((0, 0), (0, 0), (0, query_count)))]
    unnamed x194 -> x22, local copies, waits for them, and re-layouts: 136 us -> 9.22 us
    dot_general x43 -> x0, matrix products: 117 us -> none  [the longest x2 13 us: body(): jnp.einsum('ekf,efd->ekd', forward_activated, forward_down_full, preferre...]
    all_gather x7 -> x0, blocking collectives: 111 us -> none  [the longest x1 34 us: body(): lax.all_gather(qkv_weight, ('dp', 'ctx'), axis=1, tiled=True)]
    psum x3 -> x0, waiting for transfers between devices: 88 us -> none  [the longest x1 67.3 us: body(): lax.psum(spread_grad.astype(jnp.bfloat16), 'tensor').astype(jnp.float32)]
    all_gather x2 -> x0, waiting for transfers between devices: 84.8 us -> none  [the longest x1 73.8 us: body(): lax.all_gather(up_weight, ('dp', 'ctx'), axis=1, tiled=True)]
  transfers between devices with their start and end apart: 12 -> 0, of which waited for: 7 -> 0; matrix products, arithmetic and copies ran while one was open for 28% -> 0% of each run, Pallas kernels for 0% -> 0%
where the time goes in v3:
time: 310 us
  Pallas kernels  288 us (93%)
  local copies, waits for them, and re-layouts  17.3 us (6%)
  other arithmetic  3.54 us (1%)
    pallas_call x1, Pallas kernels, second_call(): pl.pallas_call(functools.partial(second_kernel, heads), out_shape=(sds((r...  154 us
    pallas_call x1, Pallas kernels, first_call(): pl.pallas_call(functools.partial(first_kernel, heads), out_shape=(sds((2,...  134 us
    unnamed x22, local copies, waits for them, and re-layouts  9.22 us

profile of v3, /device:TPU:0, one launch (start us, length us, event | category | flops | bytes accessed | tf_op | source)
XLA Modules:
  0.0 309.7 jit_solution(4093254257600507427)
XLA Ops:
  0.6 0.0 copy-start.3
  0.7 0.1 pad.11.clone
  0.8 0.8 maximum_maximum_fusion
  1.6 0.7 copy.50
  2.3 0.7 reshape_squeeze.15.slot_lanes
  3.0 1.4 copy.42.bias_ref
  4.4 0.1 dynamic_update_slice.3
  4.5 0.8 copy.33
  5.3 0.9 fusion.1
  6.2 0.1 copy.47
  6.3 0.1 copy.48
  6.5 0.1 copy.39
  6.6 0.1 copy.49
  6.7 0.8 pad_maximum_fusion.4
  7.5 0.1 copy.40
  7.6 0.7 pad_maximum_fusion.2.wsmall
  8.3 1.0 copy.51
  9.4 1.1 pad_maximum_fusion.w
  10.5 134.3 %shard_map.204 = (f32[2,128,768]{2,1,0:T(8,128)}, bf16[1024,768]{1,0:T(8,128)(2,1)}, bf16[1024,768]{1,0:T(8,128)(2,1)}, bf16[1024,384]{1,0:T(8,128)(2,1)}, bf16[...) custom-call(s32[2]{0:T(128)} %len_ref.3, ...), custom_call_target="tpu_custom_call" | custom-call | tf_op jit(solution)/shard_map/pallas_call | solution.py:460
  144.8 153.7 %shard_map.205 = (bf16[1024,768]{1,0:T(8,128)(2,1)}, bf16[1024,768]{1,0:T(8,128)(2,1)}, f32[4,2,96,768]{3,2,1,0:T(8,128)}, f32[96,768]{1,0:T(8,128)}, f32[8,768]{1,0:T(8,128)}, /*index=5*/f32[32,128]{1,0:T(8,128)}) custom-call(s32[2]{0:T(128)} %len_ref.3, f32[32,3]{1,0:T(8,128)} %copy.42.bias_ref, s32[1024,1]{1,0:T(8,128)} %bitcast.46, s32[8,256]{1,0:T(8,128)} %copy-done.5, ...), custom_call_target="tpu_custom_call" | custom-call | tf_op jit(solution)/shard_map/pallas_call | solution.py:1060
  298.6 1.5 copy.46
  300.1 0.8 constant_dynamic-slice_fusion
  300.9 0.5 slice_bitcast_fusion.3
  301.4 0.6 slice_bitcast_fusion.2
  302.0 1.1 copy.44
  303.1 0.7 fusion
  303.8 0.9 copy.45
  304.7 1.6 slice_bitcast_fusion
  306.3 0.3 copy-done.2
  306.6 1.1 copy.55
  307.8 0.8 copy-done.1
  308.6 1.1 copy.56
  (15 shorter events, 0.1 us)
Async XLA Ops:
  0.6 8.7 %copy-start.3 = (bf16[4,768,96]{1,2,0:T(8,128)(2,1)S(1)}, bf16[4,768,96]{1,2,0:T(8,128)(2,1)}, u32[]{:S(2)}) copy-start(bf16[4,768,96]{1,2,0:T(8,128)(2,1)} %param.24) | copy-start | bytes 1769476
  0.7 8.7 %copy-start.4 = (bf16[4,96,768]{2,1,0:T(8,128)(2,1)S(1)}, bf16[4,96,768]{2,1,0:T(8,128)(2,1)}, u32[]{:S(2)}) copy-start(bf16[4,96,768]{2,1,0:T(8,128)(2,1)} %param.23) | copy-start | bytes 1769476
  3.0 7.5 %copy-start.5 = (s32[8,256]{1,0:T(8,128)}, s32[8,256]{1,0:T(8,128)S(1)}, u32[]{:S(2)}) copy-start(s32[8,256]{1,0:T(8,128)S(1)} %reshape_squeeze.15.slot_lanes) | copy-start | bytes 24580
  298.6 6.1 %copy-start = (f32[4,2,96,768]{3,2,1,0:T(8,128)S(1)}, f32[4,2,96,768]{3,2,1,0:T(8,128)}, u32[]{:S(2)}) copy-start(f32[4,2,96,768]{3,2,1,0:T(8,128)} %get-tuple-element.41) | copy-start | bytes 7077892
  304.7 1.9 copy-start.2
  306.6 2.0 copy-start.1
